TPU v7x, 128 devices: a whole 4x4x4 slice. The times are simulated.
128 devices in a mesh: pipe: 2 (over core), dp: 4 (over y), tensor: 16 (over z, x).
Axes of the slice: x: 4, y: 4, z: 4, core: 2. Of those that a mesh axis runs over, the one named last changes fastest.
Arguments:
- tokens: bfloat16 [2, 1024, 1536], P(None, 'dp'), may hold values from -6 to 6
- seq_lengths: int32 [2, 2], replicated, may hold values from 1 to 769, 1024 in all within a row
- cotangent: bfloat16 [2, 1024, 1536], P(None, 'dp'), may hold values from -6 to 6
- pre_gain: float32 [2, 1536], P('pipe'), may hold values from 0.1 to 1.9
- w_z: bfloat16 [2, 1536, 3072], P('pipe', None, 'tensor'), may hold values from -0.15625 to 0.15625
- w_x: bfloat16 [2, 1536, 3072], P('pipe', None, 'tensor'), may hold values from -0.15625 to 0.15625
- w_bc: bfloat16 [2, 1536, 256], P('pipe'), may hold values from -0.15625 to 0.15625
- w_dt: bfloat16 [2, 1536, 48], P('pipe', None, 'tensor'), may hold values from -0.15625 to 0.15625
- conv_x: float32 [2, 4, 3072], P('pipe', None, 'tensor'), may hold values from -3 to 3
- conv_bc: float32 [2, 4, 256], P('pipe'), may hold values from -3 to 3
- conv_bias_x: float32 [2, 3072], P('pipe', 'tensor'), may hold values from -0.5 to 0.5
- conv_bias_bc: float32 [2, 256], P('pipe'), may hold values from -0.5 to 0.5
- dt_bias: float32 [2, 48], P('pipe', 'tensor'), may hold values from -3 to -1
- a_log: float32 [2, 48], P('pipe', 'tensor'), may hold values from -8 to -2
- d_skip: float32 [2, 48], P('pipe', 'tensor'), may hold values from 0.5 to 1.5
- inner_gain: float32 [2, 3072], P('pipe', 'tensor'), may hold values from 0.1 to 1.9
- w_out: bfloat16 [2, 3072, 1536], P('pipe', 'tensor'), may hold values from -0.109375 to 0.109375
Outputs:
- section_outputs: bfloat16 [2, 2, 1024, 1536], P('pipe', None, 'dp')
- input_grads: bfloat16 [2, 2, 1024, 1536], P('pipe', None, 'dp')
- grad_pre_gain: float32 [2, 1536], P('pipe')
- grad_w_z: float32 [2, 1536, 3072], P('pipe', None, 'tensor')
- grad_w_x: float32 [2, 1536, 3072], P('pipe', None, 'tensor')
- grad_w_bc: float32 [2, 1536, 256], P('pipe')
- grad_w_dt: float32 [2, 1536, 48], P('pipe', None, 'tensor')
- grad_conv_x: float32 [2, 4, 3072], P('pipe', None, 'tensor')
- grad_conv_bc: float32 [2, 4, 256], P('pipe')
- grad_conv_bias_x: float32 [2, 3072], P('pipe', 'tensor')
- grad_conv_bias_bc: float32 [2, 256], P('pipe')
- grad_dt_bias: float32 [2, 48], P('pipe', 'tensor')
- grad_a_log: float32 [2, 48], P('pipe', 'tensor')
- grad_d_skip: float32 [2, 48], P('pipe', 'tensor')
- grad_inner_gain: float32 [2, 3072], P('pipe', 'tensor')
- grad_w_out: float32 [2, 3072, 1536], P('pipe', 'tensor')
Inputs may be any that keep to these rules, and one draw needn't show every extreme that they name: `seq_lengths`: each row sums to 1024; its longest sequence has at most 769 tokens.
All inputs are finite; a program needn't handle non-finite values.
Results may differ from a plain program's by a relative error of at most 0.019.
Values may be sent and summed in bfloat16 or wider, within the bound.
A program may use at most 128 MiB of HBM per device.

v0:
```python
import jax
import jax.numpy as jnp
from jax import lax
from jax.sharding import PartitionSpec as P

CONV = 4
GROUP = 128
INNER = 3072


highest = lax.Precision.HIGHEST
epsilon = 1e-05


def from_behind(value, axis, steps):
    count = lax.axis_size(axis)
    first, last = (max(0, -steps), min(count, count - steps))
    return lax.ppermute(value, axis, [(source, source + steps) for source in range(first, last)])


def carried_in(value, axis, join, neutral, backward):
    count, mine = (lax.axis_size(axis), lax.axis_index(axis))
    pieces = jax.tree.map(lambda part: lax.all_gather(part, axis), value)
    if backward:
        pieces = jax.tree.map(lambda part: part[::-1], pieces)
        mine = count - 1 - mine
    total = jax.tree.map(
        lambda part, zero: jnp.full_like(part, 0) + jnp.asarray(zero, part.dtype), value, neutral
    )

    def lap(position, total):
        longer = join(total, jax.tree.map(lambda part: part[position], pieces))
        return jax.tree.map(lambda new, old: jnp.where(position < mine, new, old), longer, total)

    return lax.fori_loop(0, count - 1, lap, total)


def silu_act(signal):
    return signal * jax.nn.sigmoid(signal)


def sequence_ids(seq_lengths, positions):
    seq_ends = jnp.cumsum(seq_lengths, dtype=jnp.int32)
    counted = jnp.sum(
        (positions[:, None] >= seq_ends[None, :]).astype(jnp.int32), axis=1, dtype=jnp.int32
    )
    return jnp.where(positions < 0, -1, counted)


def causal_conv(extended, ext_ids, conv_weight, conv_bias_v, length):
    kernel_len = conv_weight.shape[0]
    current = ext_ids[kernel_len - 1 : kernel_len - 1 + length]
    summed = jnp.zeros((length, extended.shape[1]), jnp.float32) + conv_bias_v[None, :]
    for lag_rows in range(kernel_len):
        first_row = kernel_len - 1 - lag_rows
        shifted = extended[first_row : first_row + length]
        same_seq = (ext_ids[first_row : first_row + length] == current).astype(jnp.float32)
        summed = (
            summed + conv_weight[kernel_len - 1 - lag_rows][None, :] * shifted * same_seq[:, None]
        )
    return summed


def group_scan(ssm_state, group_in):
    head_block, dt_block, b_block, c_block, id_block, prior_id, rate_row = group_in
    row_count = head_block.shape[0]
    cumulative = jnp.cumsum(dt_block * rate_row[None, :], axis=0)
    order_ok = jnp.arange(row_count)[:, None] >= jnp.arange(row_count)[None, :]
    same_seq = (id_block[:, None] == id_block[None, :]) & order_ok
    differ = cumulative.T[:, :, None] - cumulative.T[:, None, :]
    decay_mat = jnp.exp(jnp.where(same_seq[None], differ, -jnp.inf))
    scores = jnp.dot(c_block, b_block.T, precision=highest)
    weights = scores[None] * decay_mat * dt_block.T[:, None, :]
    intra_out = jnp.einsum("hts,shp->thp", weights, head_block, precision=highest)
    carry_in = (id_block == prior_id).astype(jnp.float32)[:, None] * jnp.exp(cumulative)
    inter_out = (
        jnp.einsum("tn,hpn->thp", c_block, ssm_state, precision=highest) * carry_in[:, :, None]
    )
    tail_same = (id_block == id_block[row_count - 1])[:, None]
    tail_decay = (
        jnp.exp(jnp.where(tail_same, cumulative[row_count - 1][None, :] - cumulative, -jnp.inf))
        * dt_block
    )
    new_state = ssm_state * carry_in[row_count - 1][:, None, None] + jnp.einsum(
        "sh,shp,sn->hpn", tail_decay, head_block, b_block, precision=highest
    )
    return (new_state, intra_out + inter_out)


def ssd_parts(head_input, step_size, neg_rate, b_all, c_all, token_ids, prior_id):
    length, head_count, head_dim = head_input.shape
    group_count = length // GROUP
    group_ids = token_ids.reshape(group_count, GROUP)
    priors = jnp.concatenate(
        [jnp.full((1,), -1, jnp.int32), group_ids[: group_count - 1, GROUP - 1]]
    )
    rates = jnp.broadcast_to(neg_rate[None, :], (group_count, head_count))
    zero_state = jnp.zeros((head_count, head_dim, b_all.shape[1]), jnp.float32)
    blocks = (
        head_input.reshape(group_count, GROUP, head_count, head_dim),
        step_size.reshape(group_count, GROUP, head_count),
        b_all.reshape(group_count, GROUP, b_all.shape[1]),
        c_all.reshape(group_count, GROUP, c_all.shape[1]),
        group_ids,
        priors,
        rates,
    )
    final_state, outputs = lax.scan(jax.checkpoint(group_scan), zero_state, blocks)
    cumulative = jnp.cumsum(step_size * neg_rate[None, :], axis=0)
    carry_in = (token_ids == prior_id).astype(jnp.float32)[:, None] * jnp.exp(cumulative)
    return (outputs.reshape(length, head_count, head_dim), final_state, carry_in)


def add_start(scanned, carry_in, c_all, start_state):
    return (
        scanned
        + jnp.einsum("tn,hpn->thp", c_all, start_state, precision=highest) * carry_in[:, :, None]
    )


def link_states(earlier, later):
    return (earlier[0] * later[0], later[0][:, None, None] * earlier[1] + later[1])


def contract_rows(left, right):
    return lax.dot_general(
        left, right, (((0,), (0,)), ((), ())), preferred_element_type=jnp.float32
    )


def times_transposed(left, right):
    return lax.dot_general(
        left, right, (((1,), (1,)), ((), ())), preferred_element_type=jnp.float32
    )


def split_active(active, inner_local, head_count):
    length = active.shape[0]
    state_size = (active.shape[1] - inner_local) // 2
    head_input = active[:, :inner_local].reshape(length, head_count, inner_local // head_count)
    return (
        head_input,
        active[:, inner_local : inner_local + state_size],
        active[:, inner_local + state_size :],
    )


def layer_forward(hidden_in, ext_ids, params):
    (
        pre_gain,
        w_z,
        w_x,
        w_bc,
        w_dt,
        conv_x,
        conv_bc,
        conv_bias_x,
        conv_bias_bc,
        dt_bias,
        a_log,
        d_skip,
        inner_gain,
        w_out,
    ) = params
    length = hidden_in.shape[0]
    inner_local = w_x.shape[1]
    head_count = w_dt.shape[1]
    hidden = hidden_in.astype(jnp.float32)
    normed = (
        hidden
        * lax.rsqrt(jnp.mean(hidden * hidden, axis=1, keepdims=True) + epsilon)
        * pre_gain[None, :]
    ).astype(jnp.bfloat16)
    gate_pre = jnp.dot(normed, w_z, preferred_element_type=jnp.float32)
    x_pre = jnp.dot(normed, w_x, preferred_element_type=jnp.float32)
    bc_pre = jnp.dot(normed, w_bc, preferred_element_type=jnp.float32)
    dt_pre = jnp.dot(normed, w_dt, preferred_element_type=jnp.float32)
    pre_conv = jnp.concatenate([x_pre, bc_pre], axis=1)
    tails = from_behind(pre_conv[length - (CONV - 1) :], "dp", 1)
    extended = jnp.concatenate([tails, pre_conv], axis=0)
    conv_weight = jnp.concatenate([conv_x, conv_bc], axis=1)
    conv_bias_v = jnp.concatenate([conv_bias_x, conv_bias_bc])
    active = silu_act(causal_conv(extended, ext_ids, conv_weight, conv_bias_v, length))
    head_input, b_all, c_all = split_active(active, inner_local, head_count)
    step_size = jax.nn.softplus(dt_pre + dt_bias[None, :])
    neg_rate = -jnp.exp(a_log)
    token_ids = ext_ids[CONV - 1 :]
    prior_id = ext_ids[CONV - 2]
    scanned, final_state, carry_in = ssd_parts(
        head_input, step_size, neg_rate, b_all, c_all, token_ids, prior_id
    )
    identity = (jnp.ones((head_count,), jnp.float32), jnp.zeros_like(final_state))
    start_state = carried_in(
        (carry_in[length - 1], final_state), "dp", link_states, identity, False
    )[1]
    mixed_out = (
        add_start(scanned, carry_in, c_all, start_state) + d_skip[None, :, None] * head_input
    )
    gated_out = mixed_out.reshape(length, inner_local) * silu_act(gate_pre)
    square_sum = lax.psum(jnp.sum(gated_out * gated_out, axis=1), "tensor")
    inv_inner = lax.rsqrt(square_sum / INNER + epsilon)
    normed_inner = (gated_out * inv_inner[:, None] * inner_gain[None, :]).astype(jnp.bfloat16)
    partial_out = jnp.dot(normed_inner, w_out, preferred_element_type=jnp.float32)
    total_out = lax.psum(partial_out, "tensor")
    handed = (hidden + total_out).astype(jnp.bfloat16)
    saved = (hidden_in, normed, gate_pre, dt_pre, extended, ext_ids, start_state, square_sum)
    return (handed, saved)


def layer_backward(grad_out, saved, params):
    (
        pre_gain,
        w_z,
        w_x,
        w_bc,
        w_dt,
        conv_x,
        conv_bc,
        conv_bias_x,
        conv_bias_bc,
        dt_bias,
        a_log,
        d_skip,
        inner_gain,
        w_out,
    ) = params
    hidden_in, normed, gate_pre, dt_pre, extended, ext_ids, start_state, square_sum = saved
    length = hidden_in.shape[0]
    inner_local = w_x.shape[1]
    head_count = w_dt.shape[1]
    token_ids = ext_ids[CONV - 1 :]
    prior_id = ext_ids[CONV - 2]
    conv_weight = jnp.concatenate([conv_x, conv_bc], axis=1)
    conv_bias_v = jnp.concatenate([conv_bias_x, conv_bias_bc])

    def conv_piece(ext_in, weight_in, bias_in):
        return silu_act(causal_conv(ext_in, ext_ids, weight_in, bias_in, length))

    active, conv_pull = jax.vjp(conv_piece, extended, conv_weight, conv_bias_v)

    def mix_piece(state_in, active_in, dt_in, dt_bias_in, a_log_in, d_skip_in):
        head_input, b_all, c_all = split_active(active_in, inner_local, head_count)
        step_size = jax.nn.softplus(dt_in + dt_bias_in[None, :])
        neg_rate = -jnp.exp(a_log_in)
        scanned, final_state, carry_in = ssd_parts(
            head_input, step_size, neg_rate, b_all, c_all, token_ids, prior_id
        )
        mixed_out = (
            add_start(scanned, carry_in, c_all, state_in) + d_skip_in[None, :, None] * head_input
        )
        end_state = final_state + carry_in[length - 1][:, None, None] * state_in
        return ((mixed_out.reshape(length, inner_local), end_state), (carry_in, c_all))

    (mixed_flat, end_unused), mix_pull, (carry_in, c_all) = jax.vjp(
        mix_piece, start_state, active, dt_pre, dt_bias, a_log, d_skip, has_aux=True
    )
    sigmoid_gate = jax.nn.sigmoid(gate_pre)
    gated_out = mixed_flat * gate_pre * sigmoid_gate
    inv_inner = lax.rsqrt(square_sum / INNER + epsilon)
    normed_inner = (gated_out * inv_inner[:, None] * inner_gain[None, :]).astype(jnp.bfloat16)
    grad_w_out = contract_rows(normed_inner, grad_out)
    grad_normed_inner = times_transposed(grad_out, w_out)
    weighted = grad_normed_inner * inner_gain[None, :]
    grad_inner_gain = jnp.sum(grad_normed_inner * gated_out * inv_inner[:, None], axis=0)
    cross = lax.psum(jnp.sum(weighted * gated_out, axis=1), "tensor")
    grad_gated = inv_inner[:, None] * weighted - gated_out * (inv_inner**3 / INNER * cross)[:, None]
    grad_mixed = grad_gated * gate_pre * sigmoid_gate
    grad_gate = (
        grad_gated * mixed_flat * sigmoid_gate * (1.0 + gate_pre * (1.0 - sigmoid_gate))
    ).astype(jnp.bfloat16)
    grad_heads = grad_mixed.reshape(length, head_count, inner_local // head_count)
    local_grad = jnp.einsum("th,thp,tn->hpn", carry_in, grad_heads, c_all, precision=highest)
    identity = (jnp.ones((head_count,), jnp.float32), jnp.zeros_like(local_grad))
    later_grad = carried_in((carry_in[length - 1], local_grad), "dp", link_states, identity, True)[
        1
    ]
    grad_start_unused, grad_active, grad_dt_pre, grad_dt_bias, grad_a_log, grad_d_skip = mix_pull(
        (grad_mixed, later_grad)
    )
    bc_grad = lax.psum(grad_active[:, inner_local:], "tensor")
    grad_active = jnp.concatenate([grad_active[:, :inner_local], bc_grad], axis=1)
    grad_extended, grad_conv_weight, grad_conv_bias = conv_pull(grad_active)
    returned = from_behind(grad_extended[: CONV - 1], "dp", -1)
    grad_pre = grad_extended[CONV - 1 :]
    grad_pre = jnp.concatenate(
        [grad_pre[: length - (CONV - 1)], grad_pre[length - (CONV - 1) :] + returned], axis=0
    )
    grad_x_low = grad_pre[:, :inner_local].astype(jnp.bfloat16)
    grad_bc_low = grad_pre[:, inner_local:].astype(jnp.bfloat16)
    grad_dt_low = grad_dt_pre.astype(jnp.bfloat16)
    grad_w_z = contract_rows(normed, grad_gate)
    grad_w_x = contract_rows(normed, grad_x_low)
    grad_w_bc = contract_rows(normed, grad_bc_low)
    grad_w_dt = contract_rows(normed, grad_dt_low)
    partial_in = (
        times_transposed(grad_gate, w_z)
        + times_transposed(grad_x_low, w_x)
        + times_transposed(grad_dt_low, w_dt)
    )
    hidden = hidden_in.astype(jnp.float32)
    grad_normed = lax.psum(partial_in, "tensor") + times_transposed(grad_bc_low, w_bc)

    def norm_piece(hidden_v, gain_in):
        return (
            hidden_v
            * lax.rsqrt(jnp.mean(hidden_v * hidden_v, axis=1, keepdims=True) + epsilon)
            * gain_in[None, :]
        )

    norm_unused, norm_pull = jax.vjp(norm_piece, hidden, pre_gain)
    grad_hidden, grad_pre_gain = norm_pull(grad_normed)
    grad_in = grad_out.astype(jnp.float32) + grad_hidden
    grads = (
        grad_pre_gain,
        grad_w_z,
        grad_w_x,
        grad_w_bc,
        grad_w_dt,
        grad_conv_weight[:, :inner_local],
        grad_conv_weight[:, inner_local:],
        grad_conv_bias[:inner_local],
        grad_conv_bias[inner_local:],
        grad_dt_bias,
        grad_a_log,
        grad_d_skip,
        grad_inner_gain,
        grad_w_out,
    )
    return (grad_in, grads)


def on_device(
    tokens,
    seq_lengths,
    cotangent,
    pre_gain,
    w_z,
    w_x,
    w_bc,
    w_dt,
    conv_x,
    conv_bc,
    conv_bias_x,
    conv_bias_bc,
    dt_bias,
    a_log,
    d_skip,
    inner_gain,
    w_out,
):
    is_first = lax.axis_index("pipe") == 0
    rank = lax.axis_index("dp")
    micro_count, length, width = tokens.shape
    params = (
        pre_gain[0],
        w_z[0],
        w_x[0],
        w_bc[0],
        w_dt[0],
        conv_x[0],
        conv_bc[0],
        conv_bias_x[0],
        conv_bias_bc[0],
        dt_bias[0],
        a_log[0],
        d_skip[0],
        inner_gain[0],
        w_out[0],
    )
    positions = rank * length - (CONV - 1) + jnp.arange(length + CONV - 1, dtype=jnp.int32)

    def select(first_value, last_value):
        return jax.tree.map(
            lambda first_item, last_item: jnp.where(is_first, first_item, last_item),
            first_value,
            last_value,
        )

    received = jnp.zeros((length, width), jnp.bfloat16)
    handed_list = []
    saved_list = []
    inputs_list = []
    for step_index in range(micro_count + 1):
        first_micro = min(step_index, micro_count - 1)
        last_micro = max(step_index - 1, 0)
        micro_index = jnp.where(is_first, first_micro, last_micro)
        ext_ids = sequence_ids(seq_lengths[micro_index], positions)
        layer_in = jnp.where(is_first, tokens[first_micro], received)
        handed, saved = layer_forward(layer_in, ext_ids, params)
        if step_index < micro_count:
            received = from_behind(handed, "pipe", 1)
        handed_list.append(handed)
        saved_list.append(saved)
        inputs_list.append((layer_in, ext_ids))
    returned_grad = jnp.zeros((length, width), jnp.bfloat16)
    grad_list = []
    totals = None
    for step_index in range(micro_count + 1):
        last_micro = min(step_index, micro_count - 1)
        first_step = max(step_index - 1, 0)
        last_step = min(step_index + 1, micro_count)
        grad_out = jnp.where(is_first, returned_grad, cotangent[last_micro])
        layer_in, ext_ids = select(inputs_list[first_step], inputs_list[last_step])
        recomputed_unused, saved = layer_forward(layer_in, ext_ids, params)
        grad_in, grads = layer_backward(grad_out, saved, params)
        valid = jnp.where(is_first, step_index >= 1, step_index < micro_count)
        grads = jax.tree.map(
            lambda grad_item: jnp.where(valid, grad_item, jnp.zeros_like(grad_item)), grads
        )
        totals = (
            grads
            if totals is None
            else jax.tree.map(lambda left_item, right_item: left_item + right_item, totals, grads)
        )
        grad_low = grad_in.astype(jnp.bfloat16)
        grad_list.append(grad_low)
        if step_index < micro_count:
            returned_grad = from_behind(grad_low, "pipe", -1)
    (
        sum_pre_gain,
        sum_w_z,
        sum_w_x,
        sum_w_bc,
        sum_w_dt,
        sum_conv_x,
        sum_conv_bc,
        sum_bias_x,
        sum_bias_bc,
        sum_dt_bias,
        sum_a_log,
        sum_d_skip,
        sum_inner_gain,
        sum_w_out,
    ) = totals
    reduced = lax.psum(
        (
            sum_pre_gain,
            sum_w_z,
            sum_w_x,
            sum_w_bc,
            sum_w_dt,
            sum_conv_x,
            sum_conv_bc,
            sum_bias_x,
            sum_bias_bc,
            sum_dt_bias,
            sum_a_log,
            sum_d_skip,
            sum_inner_gain,
            sum_w_out,
        ),
        "dp",
    )
    section_outputs = jnp.stack(
        [
            select(handed_list[micro_index], handed_list[micro_index + 1])
            for micro_index in range(micro_count)
        ]
    )[None]
    input_grads = jnp.stack(
        [
            select(grad_list[micro_index + 1], grad_list[micro_index])
            for micro_index in range(micro_count)
        ]
    )[None]
    return (
        section_outputs,
        input_grads,
        reduced[0][None],
        reduced[1][None],
        reduced[2][None],
        reduced[3][None],
        reduced[4][None],
        reduced[5][None],
        reduced[6][None],
        reduced[7][None],
        reduced[8][None],
        reduced[9][None],
        reduced[10][None],
        reduced[11][None],
        reduced[12][None],
        reduced[13][None],
    )


def solution(mesh):
    in_specs = (
        P(None, "dp", None),
        P(),
        P(None, "dp", None),
        P("pipe", None),
        P("pipe", None, "tensor"),
        P("pipe", None, "tensor"),
        P("pipe", None, None),
        P("pipe", None, "tensor"),
        P("pipe", None, "tensor"),
        P("pipe", None, None),
        P("pipe", "tensor"),
        P("pipe", None),
        P("pipe", "tensor"),
        P("pipe", "tensor"),
        P("pipe", "tensor"),
        P("pipe", "tensor"),
        P("pipe", "tensor", None),
    )
    out_specs = (
        P("pipe", None, "dp", None),
        P("pipe", None, "dp", None),
        P("pipe", None),
        P("pipe", None, "tensor"),
        P("pipe", None, "tensor"),
        P("pipe", None, None),
        P("pipe", None, "tensor"),
        P("pipe", None, "tensor"),
        P("pipe", None, None),
        P("pipe", "tensor"),
        P("pipe", None),
        P("pipe", "tensor"),
        P("pipe", "tensor"),
        P("pipe", "tensor"),
        P("pipe", "tensor"),
        P("pipe", "tensor", None),
    )
    return jax.shard_map(
        on_device, mesh=mesh, in_specs=in_specs, out_specs=out_specs, check_vma=False
    )
```

profile of v0, /device:TPU:0, one launch (start us, length us, event | category | flops | bytes accessed | tf_op | source)
XLA Modules:
  0.0 2004.6 jit_solution(1737702440998373761)
XLA Ops:
  13.6 4.4 collective-permute-start
  26.8 8.1 all-gather.9
  40.0 22.4 %while.327 = (s32[]{:T(128)}, f32[3,64,128]{2,1,0:T(8,128)S(1)}, f32[2,128,3,64]{1,0,3,2:T(2,128)}, s32[2,128]{1,0:T(2,128)}, s32[2]{0:T(128)}, /*index=5*/f32[2...) while((s32[]{:T(128)}, f32[3,64,128]{2,1,0:T(8,128)S(1)}, ...), condition=%wide.region_5.6_spmd.clone, body=%wide.region_3.5_spmd.clone.sunk | while | flops 138880896 | bytes 1645620 | solution.py:108
  47.6 3.5 dynamic_update_slice.254
  58.8 3.5 dynamic_update_slice.254
  64.2 12.6 all-gather
  82.2 41.7 %psum.224 = f32[256]{0:T(256)S(1)} all-reduce(f32[256]{0:T(256)S(1)} %get-tuple-element.4596), channel_id=1, replica_groups=mesh['pipe'=2,'dp'=4,'tensor'=16] {'tensor'}, use_global_device_ids=true, to_apply=%region_11.12 | all-reduce | flops 256 | bytes 2048 | tf_op jit(solution)/shard_map/psum | solution.py:200
  129.3 79.8 %all-reduce.59.cloned.1.call-done = f32[256,1536]{1,0:T(8,128)} async-done(((f32[256,1536]{1,0:T(8,128)}), f32[256,1536]{1,0:T(8,128)}) %all-reduce.59.cloned.1.call-update) | async-done | bytes 1572880 | tf_op jit(solution)/shard_map/psum | solution.py:204
  224.0 4.1 collective-permute-start.5
  233.9 7.7 all-gather.12
  241.6 8.6 all-gather.10
  263.4 25.9 %while.335 = (s32[]{:T(128)}, f32[3,64,128]{2,1,0:T(8,128)S(1)}, f32[2,128,3,64]{1,0,3,2:T(2,128)}, f32[2,3,64,128]{3,2,1,0:T(8,128)S(1)}, s32[2,128]{1,0:T(2,12...) while((s32[]{:T(128)}, f32[3,64,128]{2,1,0:T(8,128)S(1)}, ...), condition=%wide.region_51.53_spmd.clone, body=%wide.region_49.52_spmd.clone.sunk | while | flops 138905472 | bytes 3418240 | solution.py:108
  291.2 24.1 %while.333 = (s32[]{:T(128)}, f32[3,64,128]{2,1,0:T(8,128)S(1)}, f32[2,128,3,64]{1,0,3,2:T(2,128)S(1)}, s32[2,128]{1,0:T(2,128)}, s32[2]{0:T(128)}, /*index=5*/f...) while((s32[]{:T(128)}, f32[3,64,128]{2,1,0:T(8,128)S(1)}, ...), condition=%wide.region_42.43_spmd.clone, body=%wide.region_40.42_spmd.clone.sunk | while | flops 138880896 | bytes 1452091 | solution.py:108
  316.1 12.6 all-gather.3
  334.3 14.8 while.329
  349.3 13.4 all-gather.1
  362.7 5.0 while.330
  373.6 38.3 %all-reduce.45 = (f32[256]{0:T(256)S(1)}, f32[256]{0:T(256)S(1)}) all-reduce(f32[256]{0:T(256)} %get-tuple-element.4601, f32[256]{0:T(256)} %get-tuple-element.4539), channel_id=1, replica_groups=mesh['pipe'=2,'dp'=4,'tensor'=16] {'tensor'}, use_global_device_ids=true, to_apply=%region_24.25 | all-reduce | flops 512 | bytes 4096 | tf_op jit(solution)/shard_map/psum | solution.py:200
  428.0 71.1 %all-reduce.61.cloned.1.call-done = f32[256,1536]{1,0:T(8,128)} async-done(((f32[256,1536]{1,0:T(8,128)}), f32[256,1536]{1,0:T(8,128)}) %all-reduce.61.cloned.1.call-update) | async-done | bytes 1572880 | tf_op jit(solution)/shard_map/psum | solution.py:204
  505.9 10.0 all-gather.13
  533.8 7.4 all-gather.14
  544.8 4.2 collective-permute-start.11
  552.5 7.3 all-gather.16
  560.7 9.0 all-gather.15
  577.3 7.5 all-gather.11
  600.9 37.5 %while.339 = (s32[]{:T(128)}, f32[3,64,128]{2,1,0:T(8,128)}, f32[2,128,3,64]{1,0,3,2:T(2,128)}, f32[2,3,64,128]{3,2,1,0:T(8,128)}, s32[2,128]{1,0:T(2,128)}, /*i...) while((s32[]{:T(128)}, f32[3,64,128]{2,1,0:T(8,128)}, ...), condition=%wide.region_89.91_spmd.clone, body=%wide.region_87.90_spmd.clone.sunk | while | flops 138905472 | bytes 1851492 | solution.py:108
  615.4 3.5 dynamic_update_slice.262
  640.9 36.2 %while.337 = (s32[]{:T(128)}, f32[3,64,128]{2,1,0:T(8,128)}, f32[2,128,3,64]{1,0,3,2:T(2,128)}, s32[2,128]{1,0:T(2,128)}, s32[2]{0:T(128)}, /*index=5*/f32[2,128...) while((s32[]{:T(128)}, f32[3,64,128]{2,1,0:T(8,128)}, ...), condition=%wide.region_80.82_spmd.clone, body=%wide.region_78.81_spmd.clone.sunk | while | flops 138880896 | bytes 1654871 | solution.py:108
  677.1 13.0 all-gather.5
  690.2 8.2 while.338
  704.4 38.9 %all-reduce.44 = (f32[256]{0:T(256)S(1)}, f32[256]{0:T(256)}) all-reduce(f32[256]{0:T(256)S(1)} %copy-done.347, f32[256]{0:T(256)S(1)} %get-tuple-element.4537), channel_id=1, replica_groups=mesh['pipe'=2,'dp'=4,'tensor'=16] {'tensor'}, use_global_device_ids=true, to_apply=%region_55.57 | all-reduce | flops 512 | bytes 4096 | tf_op jit(solution)/shard_map/psum | solution.py:265
  747.2 13.3 all-gather.4
  762.3 5.0 while.336
  770.6 95.2 %while.324 = (s32[]{:T(128)}, f32[3,64,128]{2,1,0:T(8,128)S(1)}, f32[2,128,3,64]{1,0,3,2:T(2,128)}, f32[2,128,3]{1,2,0:T(4,128)}, f32[2,128,128]{2,1,0:T(8,128)}...) while((s32[]{:T(128)}, f32[3,64,128]{2,1,0:T(8,128)S(1)}, ...), condition=%wide.region_69.71_spmd, body=%wide.region_58.70_spmd.sunk | while | flops 341065216 | bytes 4556757 | solution.py:108
  879.2 3.8 reduce-window.126
  891.5 9.0 all-gather.17
  906.0 52.0 %all-reduce.63.cloned.1.call-done = f32[256,256]{0,1:T(8,128)} async-done(((f32[256,256]{0,1:T(8,128)}), f32[256,256]{0,1:T(8,128)}) %all-reduce.63.cloned.1.call-update) | async-done | bytes 262160 | tf_op jit(solution)/shard_map/psum | solution.py:280
  973.7 37.5 %while.343 = (s32[]{:T(128)}, f32[3,64,128]{2,1,0:T(8,128)}, f32[2,128,3,64]{1,0,3,2:T(2,128)}, f32[2,3,64,128]{3,2,1,0:T(8,128)}, s32[2,128]{1,0:T(2,128)}, /*i...) while((s32[]{:T(128)}, f32[3,64,128]{2,1,0:T(8,128)}, ...), condition=%wide.region_127.129_spmd.clone, body=%wide.region_125.128_spmd.clone.sunk | while | flops 138905472 | bytes 1851492 | solution.py:108
  1018.7 36.2 %while.341 = (s32[]{:T(128)}, f32[3,64,128]{2,1,0:T(8,128)}, f32[2,128,3,64]{1,0,3,2:T(2,128)}, s32[2,128]{1,0:T(2,128)}, s32[2]{0:T(128)}, /*index=5*/f32[2,128...) while((s32[]{:T(128)}, f32[3,64,128]{2,1,0:T(8,128)}, ...), condition=%wide.region_118.120_spmd.clone, body=%wide.region_116.119_spmd.clone.sunk | while | flops 138880896 | bytes 1654871 | solution.py:108
  1054.9 17.0 all-gather.7
  1073.0 34.9 %all-reduce.65.cloned.1.call-done = f32[256,1536]{1,0:T(8,128)} async-done(((f32[256,1536]{1,0:T(8,128)}), f32[256,1536]{1,0:T(8,128)}) %all-reduce.65.cloned.1.call-update) | async-done | bytes 1572880 | tf_op jit(solution)/shard_map/psum | solution.py:301
  1113.8 4.9 while.342
  1130.1 38.8 %all-reduce.43 = (f32[256]{0:T(256)S(1)}, f32[256]{0:T(256)}) all-reduce(f32[256]{0:T(256)S(1)} %get-tuple-element.3988, f32[256]{0:T(256)S(1)} %get-tuple-element.4535), channel_id=1, replica_groups=mesh['pipe'=2,'dp'=4,'tensor'=16] {'tensor'}, use_global_device_ids=true, to_apply=%region_93.95 | all-reduce | flops 512 | bytes 4096 | tf_op jit(solution)/shard_map/psum | solution.py:265
  1172.9 14.0 all-gather.6
  1188.7 4.9 while.340
  1196.8 95.0 %while.325 = (s32[]{:T(128)}, f32[3,64,128]{2,1,0:T(8,128)S(1)}, f32[2,128,3,64]{1,0,3,2:T(2,128)}, f32[2,128,3]{1,2,0:T(4,128)}, f32[2,128,128]{2,1,0:T(8,128)}...) while((s32[]{:T(128)}, f32[3,64,128]{2,1,0:T(8,128)S(1)}, ...), condition=%wide.region_107.109_spmd, body=%wide.region_96.108_spmd.sunk | while | flops 341065216 | bytes 4556757 | solution.py:108
  1307.0 3.8 reduce-window.163
  1317.0 68.6 %all-reduce.67.cloned.1.call-done = f32[256,256]{0,1:T(8,128)} async-done(((f32[256,256]{0,1:T(8,128)}), f32[256,256]{0,1:T(8,128)}) %all-reduce.67.cloned.1.call-update) | async-done | bytes 262160 | tf_op jit(solution)/shard_map/psum | solution.py:280
  1405.3 36.6 %while.331 = (s32[]{:T(128)}, f32[3,64,128]{2,1,0:T(8,128)S(1)}, f32[2,128,3,64]{1,0,3,2:T(2,128)}, s32[2,128]{1,0:T(2,128)S(1)}, s32[2]{0:T(128)S(1)}, /*index=...) while((s32[]{:T(128)}, f32[3,64,128]{2,1,0:T(8,128)S(1)}, ...), condition=%wide.region_31.32_spmd.clone, body=%wide.region_29.31_spmd.clone.sunk | while | flops 138880896 | bytes 1650268 | solution.py:108
  1438.3 3.6 dynamic_update_slice.256
  1441.9 13.6 all-gather.2
  1455.5 37.6 %all-reduce.69.cloned.1.call-done = f32[256,1536]{1,0:T(8,128)} async-done(((f32[256,1536]{1,0:T(8,128)}), f32[256,1536]{1,0:T(8,128)}) %all-reduce.69.cloned.1.call-update) | async-done | bytes 1572880 | tf_op jit(solution)/shard_map/psum | solution.py:301
  1499.4 4.9 while.332
  1514.0 38.8 %all-reduce.42 = (f32[256]{0:T(256)}, f32[256]{0:T(256)S(1)}) all-reduce(f32[256]{0:T(256)S(1)} %get-tuple-element.4612, f32[256]{0:T(256)S(1)} %get-tuple-element.3990), channel_id=1, replica_groups=mesh['pipe'=2,'dp'=4,'tensor'=16] {'tensor'}, use_global_device_ids=true, to_apply=%region_37.38 | all-reduce | flops 512 | bytes 4096 | tf_op jit(solution)/shard_map/psum | solution.py:200
  1556.8 13.6 all-gather.8
  1572.2 5.0 while.344
  1580.5 94.6 %while.326 = (s32[]{:T(128)}, f32[3,64,128]{2,1,0:T(8,128)S(1)}, f32[2,128,3,64]{1,0,3,2:T(2,128)}, f32[2,128,3]{1,2,0:T(4,128)}, f32[2,128,128]{2,1,0:T(8,128)}...) while((s32[]{:T(128)}, f32[3,64,128]{2,1,0:T(8,128)S(1)}, ...), condition=%wide.region_145.147_spmd, body=%wide.region_134.146_spmd.sunk | while | flops 341065216 | bytes 4556757 | solution.py:108
  1689.9 3.8 reduce-window.169
  1699.3 69.7 %all-reduce.71.cloned.1.call-done = f32[256,256]{0,1:T(8,128)} async-done(((f32[256,256]{0,1:T(8,128)}), f32[256,256]{0,1:T(8,128)}) %all-reduce.71.cloned.1.call-update) | async-done | bytes 262160 | tf_op jit(solution)/shard_map/psum | solution.py:280
  1775.5 5.8 collective-permute-done.12
  1810.4 68.8 %all-reduce.73.cloned.1.call-done = (f32[256,1536]{1,0:T(8,128)}, f32[256,1536]{1,0:T(8,128)}) async-done(((f32[256,1536]{1,0:T(8,128)}, f32[256,1536]{1,0:T(8,128)}), (f32[256,1536]{1,0:T(8,128)}, f32[256,1536]{1,0:T(8,128)})) %all-reduce.73.cloned.1.call-update) | async-done | bytes 3145744 | tf_op jit(solution)/shard_map/psum | solution.py:204
  1879.2 3.9 fusion.461
  1883.2 18.9 all-reduce.47
  1909.1 81.4 %all-reduce.75.cloned.1.call-done = (f32[1,1536,192]{1,2,0:T(8,128)}, f32[1,1536,192]{1,2,0:T(8,128)}, f32[1,1536,256]{2,1,0:T(8,128)}, f32[1,192,1536]{2,1,0:T(8,128)}) async-done(((f32[1,1536,192]{1,2,0:T(8,128)}, f32[1,1536,192]{1,2,0:T(8,128)}, f32[1,1536,256]{2,1,0:T(8,128)}, f32[1,192,1536]{2,1,0:T(8,128)}), (f32[1,1536,192]{1,2,0:T(8,128)}, f32[1,1536,192]{1,2,0:T(8,128)}, f32[1,1536,256]{2,1,0:T(8,128)}, ...) | async-done | bytes 5111824 | tf_op jit(solution)/shard_map/psum | solution.py:435
  (1953 shorter events, 964.2 us)
Async XLA Ops:
  7.2 201.9 %all-reduce.59.cloned.1.call-start = ((), (), s32[]{:S(2)}) async-start(), calls=%async_computation | async-start | bytes 3145728 | tf_op jit(solution)/shard_map/psum | solution.py:204
  13.6 21.4 %collective-permute-start = (f32[3,448]{0,1:T(8,128)}, f32[3,448]{0,1:T(8,128)}, u32[]{:S(2)}, u32[]{:S(2)}) collective-permute-start(f32[3,448]{0,1:T(8,128)} %fusion.607), channel_id=1, source_target_pairs={{0,16},{16,32},{32,48},{1,17},{17,33},{33,49},{2,18},{18,34},{34,5... | collective-permute-start | bytes 16136 | tf_op jit(solution)/shard_map/ppermute | solution.py:18
  25.2 564.5 %copy-start.159 = (f32[1,448]{1,0:T(1,128)}, f32[1,448]{1,0:T(1,128)S(1)}, u32[]{:S(2)}) copy-start(f32[1,448]{1,0:T(1,128)S(1)} %get-tuple-element.4543) | copy-start | bytes 5380
  25.2 564.5 %copy-start.163 = (f32[1,448]{1,0:T(1,128)}, f32[1,448]{1,0:T(1,128)S(1)}, u32[]{:S(2)}) copy-start(f32[1,448]{1,0:T(1,128)S(1)} %get-tuple-element.4544) | copy-start | bytes 5380
  80.6 43.4 %copy-start.36 = (bf16[1,192,1536]{2,1,0:T(8,128)(2,1)S(1)}, bf16[1,192,1536]{2,1,0:T(8,128)(2,1)}, u32[]{:S(2)}) copy-start(bf16[1,192,1536]{2,1,0:T(8,128)(2,1)} %param.76) | copy-start | bytes 1769476
  80.6 43.4 %copy-start.197 = (f32[1,192]{1,0:T(1,128)S(1)}, f32[1,192]{1,0:T(1,128)}, u32[]{:S(2)}) copy-start(f32[1,192]{1,0:T(1,128)} %param.75) | copy-start | bytes 2308
  125.6 373.5 %all-reduce.61.cloned.1.call-start = ((), (), s32[]{:S(2)}) async-start(), calls=%async_computation.1 | async-start | bytes 3145728 | tf_op jit(solution)/shard_map/psum | solution.py:204
  210.8 7.1 collective-permute-start.1
  219.8 34.3 %copy-start.62 = (f32[256,256]{0,1:T(8,128)}, f32[256,256]{0,1:T(8,128)S(1)}, u32[]{:S(2)}) copy-start(f32[256,256]{0,1:T(8,128)S(1)} %fusion.512) | copy-start | bytes 786436
  220.3 33.8 %copy-start.77 = (f32[256,192]{0,1:T(8,128)}, f32[256,192]{0,1:T(8,128)S(1)}, u32[]{:S(2)}) copy-start(f32[256,192]{0,1:T(8,128)S(1)} %fusion.556) | copy-start | bytes 589828
  223.9 30.3 %copy-start.268 = (f32[256]{0:T(256)S(1)}, f32[256]{0:T(256)}, u32[]{:S(2)}) copy-start(f32[256]{0:T(256)} %get-tuple-element.4572) | copy-start | bytes 3076
  223.9 30.3 %copy-start.270 = (f32[256]{0:T(256)S(1)}, f32[256]{0:T(256)}, u32[]{:S(2)}) copy-start(f32[256]{0:T(256)} %get-tuple-element.4573) | copy-start | bytes 3076
  223.9 30.3 %copy-start.272 = (f32[256]{0:T(256)S(1)}, f32[256]{0:T(256)}, u32[]{:S(2)}) copy-start(f32[256]{0:T(256)} %get-tuple-element.4574) | copy-start | bytes 3076
  224.0 28.9 %collective-permute-start.5 = (f32[3,448]{0,1:T(8,128)S(1)}, f32[3,448]{0,1:T(8,128)}, u32[]{:S(2)}, u32[]{:S(2)}) collective-permute-start(f32[3,448]{0,1:T(8,128)S(1)} %fusion.604), channel_id=1, source_target_pairs={{0,16},{16,32},{32,48},{1,17},{17,33},{33,49},{2,18},{18,34},{34,5... | collective-permute-start | bytes 16136 | tf_op jit(solution)/shard_map/ppermute | solution.py:18
  250.5 6.6 collective-permute-start.2
  371.8 144.7 %copy-start.148 = (f32[256,3,64]{0,2,1:T(8,128)}, f32[256,3,64]{0,2,1:T(8,128)S(1)}, u32[]{:S(2)}) copy-start(f32[256,3,64]{0,2,1:T(8,128)S(1)} %get-tuple-element.4526) | copy-start | bytes 589828
  371.9 40.1 %copy-start.37 = (bf16[1,192,1536]{2,1,0:T(8,128)(2,1)S(1)}, bf16[1,192,1536]{2,1,0:T(8,128)(2,1)}, u32[]{:S(2)}) copy-start(bf16[1,192,1536]{2,1,0:T(8,128)(2,1)} %param.76) | copy-start | bytes 1769476
  373.6 142.9 %copy-start.156 = (f32[256,192]{0,1:T(8,128)}, f32[256,192]{0,1:T(8,128)S(1)}, u32[]{:S(2)}) copy-start(f32[256,192]{0,1:T(8,128)S(1)} %get-tuple-element.4603) | copy-start | bytes 589828
  411.9 104.6 %copy-start.322 = (f32[256]{0:T(256)}, f32[256]{0:T(256)S(1)}, u32[]{:S(2)}) copy-start(f32[256]{0:T(256)S(1)} %get-tuple-element.4373) | copy-start | bytes 3076
  414.6 543.4 %all-reduce.63.cloned.1.call-start = ((), (), s32[]{:S(2)}) async-start(), calls=%async_computation.2 | async-start | bytes 524288 | tf_op jit(solution)/shard_map/psum | solution.py:280
  421.0 81.2 %copy-start.280 = (s32[2,128]{1,0:T(2,128)}, s32[2,128]{1,0:T(2,128)S(1)}, u32[]{:S(2)}) copy-start(s32[2,128]{1,0:T(2,128)S(1)} %slice_bitcast_fusion.26) | copy-start | bytes 3076
  426.7 115.8 %copy-start.276 = (f32[256]{0:T(256)}, f32[256]{0:T(256)S(1)}, u32[]{:S(2)}) copy-start(f32[256]{0:T(256)S(1)} %get-tuple-element.4563) | copy-start | bytes 3076
  428.0 77.7 %copy-start.193 = (f32[256,3]{0,1:T(4,128)S(1)}, f32[256,3]{0,1:T(4,128)}, u32[]{:S(2)}) copy-start(f32[256,3]{0,1:T(4,128)} %fusion.718) | copy-start | bytes 9220
  428.0 88.6 %copy-start.198 = (f32[1,192]{1,0:T(1,128)S(1)}, f32[1,192]{1,0:T(1,128)}, u32[]{:S(2)}) copy-start(f32[1,192]{1,0:T(1,128)} %param.75) | copy-start | bytes 2308
  502.2 17.3 collective-permute-start.3
  529.0 59.2 %collective-permute-start.8 = (f32[3,448]{0,1:T(8,128)}, f32[3,448]{0,1:T(8,128)}, u32[]{:S(2)}, u32[]{:S(2)}) collective-permute-start(f32[3,448]{0,1:T(8,128)} %fusion.603), channel_id=1, source_target_pairs={{0,16},{16,32},{32,48},{1,17},{17,33},{33,49},{2,18},{18,34},{34,5... | collective-permute-start | bytes 16136 | tf_op jit(solution)/shard_map/ppermute | solution.py:18
  544.8 44.8 %copy-start.65 = (f32[256,256]{0,1:T(8,128)S(1)}, f32[256,256]{0,1:T(8,128)}, u32[]{:S(2)}) copy-start(f32[256,256]{0,1:T(8,128)} %copy-done.64) | copy-start | bytes 786436
  544.8 344.3 %collective-permute-start.11 = (f32[3,448]{0,1:T(8,128)}, f32[3,448]{0,1:T(8,128)}, u32[]{:S(2)}, u32[]{:S(2)}) collective-permute-start(f32[3,448]{0,1:T(8,128)} %fusion.602), channel_id=1, source_target_pairs={{0,16},{16,32},{32,48},{1,17},{17,33},{33,49},{2,18},{18,34},{34,5... | collective-permute-start | bytes 16136 | tf_op jit(solution)/shard_map/ppermute | solution.py:18
  571.5 329.7 %collective-permute-start.4 = (f32[3,448]{0,1:T(8,128)}, f32[3,448]{0,1:T(8,128)}, u32[]{:S(2)}, u32[]{:S(2)}) collective-permute-start(f32[3,448]{0,1:T(8,128)} %fusion.605), channel_id=1, source_target_pairs={{0,16},{16,32},{32,48},{1,17},{17,33},{33,49},{2,18},{18,34},{34,5... | collective-permute-start | bytes 16136 | tf_op jit(solution)/shard_map/ppermute | solution.py:18
  702.0 41.3 %copy-start.323 = (f32[256]{0:T(256)S(1)}, f32[256]{0:T(256)}, u32[]{:S(2)}) copy-start(f32[256]{0:T(256)} %copy-done.322) | copy-start | bytes 3076
  702.0 41.3 %copy-start.199 = (f32[1,192]{1,0:T(1,128)S(1)}, f32[1,192]{1,0:T(1,128)}, u32[]{:S(2)}) copy-start(f32[1,192]{1,0:T(1,128)} %param.75) | copy-start | bytes 2308
  702.0 41.3 %copy-start.328 = (f32[256]{0:T(256)S(1)}, f32[256]{0:T(256)}, u32[]{:S(2)}) copy-start(f32[256]{0:T(256)} %copy-done.327) | copy-start | bytes 3076
  702.0 44.0 %copy-start.194 = (f32[256,3]{0,1:T(4,128)S(1)}, f32[256,3]{0,1:T(4,128)}, u32[]{:S(2)}) copy-start(f32[256,3]{0,1:T(4,128)} %fusion.718) | copy-start | bytes 9220
  704.4 57.9 %copy-start.56 = (f32[3,64,128]{2,1,0:T(8,128)S(1)}, f32[3,64,128]{2,1,0:T(8,128)}, u32[]{:S(2)}) copy-start(f32[3,64,128]{2,1,0:T(8,128)} %custom-call.9) | copy-start | bytes 294916
  878.2 229.7 %all-reduce.65.cloned.1.call-start = ((), (), s32[]{:S(2)}) async-start(), calls=%async_computation.3 | async-start | bytes 3145728 | tf_op jit(solution)/shard_map/psum | solution.py:301
  889.1 234.4 %copy-start.195 = (f32[256,3]{0,1:T(4,128)}, f32[256,3]{0,1:T(4,128)S(1)}, u32[]{:S(2)}) copy-start(f32[256,3]{0,1:T(4,128)S(1)} %fusion.701) | copy-start | bytes 9220
  901.3 56.7 %copy-start.63 = (f32[256,256]{0,1:T(8,128)S(1)}, f32[256,256]{0,1:T(8,128)}, u32[]{:S(2)}) copy-start(f32[256,256]{0,1:T(8,128)} %copy-done.62) | copy-start | bytes 786436
  901.3 56.7 %copy-start.269 = (f32[256]{0:T(256)S(1)}, f32[256]{0:T(256)}, u32[]{:S(2)}) copy-start(f32[256]{0:T(256)} %get-tuple-element.4572) | copy-start | bytes 3076
  965.3 47.2 %collective-permute-start.6 = (f32[3,448]{0,1:T(8,128)}, f32[3,448]{0,1:T(8,128)}, u32[]{:S(2)}, u32[]{:S(2)}) collective-permute-start(f32[3,448]{0,1:T(8,128)} %slice.1006), channel_id=1, source_target_pairs={{16,0},{32,16},{48,32},{17,1},{33,17},{49,33},{18,2},{34,18},{50,3... | collective-permute-start | bytes 16136 | tf_op jit(solution)/shard_map/ppermute | solution.py:18
  1017.9 367.7 %all-reduce.67.cloned.1.call-start = ((), (), s32[]{:S(2)}) async-start(), calls=%async_computation.4 | async-start | bytes 524288 | tf_op jit(solution)/shard_map/psum | solution.py:280
  1018.7 89.2 %copy-start.224 = (f32[256]{0:T(256)S(1)}, f32[256]{0:T(256)}, u32[]{:S(2)}) copy-start(f32[256]{0:T(256)} %copy-done.222) | copy-start | bytes 3076
  1073.0 37.9 %copy-start.121 = (bf16[256,256]{0,1:T(8,128)(2,1)}, bf16[256,256]{0,1:T(8,128)(2,1)S(1)}, u32[]{:S(2)}) copy-start(bf16[256,256]{0,1:T(8,128)(2,1)S(1)} %fusion.601) | copy-start | bytes 393220
  1073.0 37.9 %copy-start.289 = (f32[256]{0:T(256)S(1)}, f32[256]{0:T(256)}, u32[]{:S(2)}) copy-start(f32[256]{0:T(256)} %copy-done.288) | copy-start | bytes 3076
  1112.3 13.8 collective-permute-start.7
  1127.5 41.4 %copy-start.320 = (f32[256]{0:T(256)S(1)}, f32[256]{0:T(256)}, u32[]{:S(2)}) copy-start(f32[256]{0:T(256)} %get-tuple-element.4371) | copy-start | bytes 3076
  1128.4 43.2 %copy-start.191 = (f32[256,3]{0,1:T(4,128)S(1)}, f32[256,3]{0,1:T(4,128)}, u32[]{:S(2)}) copy-start(f32[256,3]{0,1:T(4,128)} %fusion.709) | copy-start | bytes 9220
  1130.1 58.6 %copy-start.53 = (f32[3,64,128]{2,1,0:T(8,128)S(1)}, f32[3,64,128]{2,1,0:T(8,128)}, u32[]{:S(2)}) copy-start(f32[3,64,128]{2,1,0:T(8,128)} %custom-call.13) | copy-start | bytes 294916
  1304.7 80.9 %copy-start.79 = (f32[256,192]{0,1:T(8,128)S(1)}, f32[256,192]{0,1:T(8,128)}, u32[]{:S(2)}) copy-start(f32[256,192]{0,1:T(8,128)} %copy-done.78) | copy-start | bytes 589828
  1305.4 187.7 %all-reduce.69.cloned.1.call-start = ((), (), s32[]{:S(2)}) async-start(), calls=%async_computation.5 | async-start | bytes 3145728 | tf_op jit(solution)/shard_map/psum | solution.py:301
  1391.2 8.2 collective-permute-start.9
  1404.3 364.6 %all-reduce.71.cloned.1.call-start = ((), (), s32[]{:S(2)}) async-start(), calls=%async_computation.6 | async-start | bytes 524288 | tf_op jit(solution)/shard_map/psum | solution.py:280
  1405.3 87.8 %copy-start.220 = (f32[256]{0:T(256)S(1)}, f32[256]{0:T(256)}, u32[]{:S(2)}) copy-start(f32[256]{0:T(256)} %copy-done.218) | copy-start | bytes 3076
  1455.5 40.5 %copy-start.285 = (f32[256]{0:T(256)S(1)}, f32[256]{0:T(256)}, u32[]{:S(2)}) copy-start(f32[256]{0:T(256)} %copy-done.284) | copy-start | bytes 3076
  1498.0 12.1 collective-permute-start.10
  1511.4 41.4 %copy-start.321 = (f32[256]{0:T(256)S(1)}, f32[256]{0:T(256)}, u32[]{:S(2)}) copy-start(f32[256]{0:T(256)} %get-tuple-element.4369) | copy-start | bytes 3076
  1512.3 43.2 %copy-start.196 = (f32[256,3]{0,1:T(4,128)S(1)}, f32[256,3]{0,1:T(4,128)}, u32[]{:S(2)}) copy-start(f32[256,3]{0,1:T(4,128)} %copy-done.195) | copy-start | bytes 9220
  1514.0 58.1 %copy-start.50 = (f32[3,64,128]{2,1,0:T(8,128)S(1)}, f32[3,64,128]{2,1,0:T(8,128)}, u32[]{:S(2)}) copy-start(f32[3,64,128]{2,1,0:T(8,128)} %custom-call.17) | copy-start | bytes 294916
  1688.7 190.5 %all-reduce.73.cloned.1.call-start = ((), (), s32[]{:S(2)}) async-start(), calls=%async_computation.7 | async-start | bytes 6291456 | tf_op jit(solution)/shard_map/psum | solution.py:204
  1696.8 72.2 %copy-start.61 = (f32[256,256]{0,1:T(8,128)S(1)}, f32[256,256]{0,1:T(8,128)}, u32[]{:S(2)}) copy-start(f32[256,256]{0,1:T(8,128)} %copy-done.59) | copy-start | bytes 786436
  1696.8 72.2 %copy-start.260 = (f32[256]{0:T(256)S(1)}, f32[256]{0:T(256)}, u32[]{:S(2)}) copy-start(f32[256]{0:T(256)} %get-tuple-element.4560) | copy-start | bytes 3076
  1696.8 72.2 %copy-start.262 = (f32[256]{0:T(256)S(1)}, f32[256]{0:T(256)}, u32[]{:S(2)}) copy-start(f32[256]{0:T(256)} %get-tuple-element.4561) | copy-start | bytes 3076
  1696.8 72.2 %copy-start.264 = (f32[256]{0:T(256)S(1)}, f32[256]{0:T(256)}, u32[]{:S(2)}) copy-start(f32[256]{0:T(256)} %get-tuple-element.4562) | copy-start | bytes 3076
  1773.2 8.1 collective-permute-start.12
  1783.8 206.7 %all-reduce.75.cloned.1.call-start = ((), (), s32[]{:S(2)}) async-start(), calls=%async_computation.8 | async-start | bytes 10223616 | tf_op jit(solution)/shard_map/psum | solution.py:435
  (338 other events, 1894.1 us)
Sparse Core Ops, SparseCore 0:
  125.7 83.3 all-reduce.58
  414.7 84.3 all-reduce.60
  878.3 79.5 all-reduce.62
  1018.1 89.8 all-reduce.64
  1305.5 80.0 all-reduce.66
  1404.4 88.5 all-reduce.68
  1688.9 80.0 all-reduce.70
  1783.9 95.2 all-reduce.72
  1883.1 107.3 all-reduce.74
where the time goes:
time: 2030 us; the launch traced here: 2000 us
  waiting for transfers between devices  571 us (28%)
  local copies, waits for them, and re-layouts  419 us (21%)
  blocking collectives  413 us (20%)
  other arithmetic  287 us (14%)
  matrix products  262 us (13%)
  starting transfers between devices  31.3 us (2%)
    psum x3, waiting for transfers between devices, layer_forward(): total_out = lax.psum(partial_out, 'tensor')  220 us
    all_gather x18, blocking collectives, carried_in(): pieces = jax.tree.map(lambda part: lax.all_gather(part, axis), value)  198 us
    psum x3, waiting for transfers between devices, layer_backward(): bc_grad = lax.psum(grad_active[:, inner_local:], 'tensor')  190 us
    psum x3, blocking collectives, layer_forward(): square_sum = lax.psum(jnp.sum(gated_out * gated_out, axis=1), 'tensor')  119 us
    dynamic_update_slice x30, local copies, waits for them, and re-layouts, ssd_parts(): lax.scan(jax.checkpoint(group_scan), zero_state, blocks)  83.4 us
    psum x1, waiting for transfers between devices, on_device(): lax.psum((sum_pre_gain, sum_w_z, sum_w_x, sum_w_bc, sum_w_dt, sum_conv_x,...  81.4 us
    psum x2, blocking collectives, layer_backward(): cross = lax.psum(jnp.sum(weighted * gated_out, axis=1), 'tensor')  77.7 us
    psum x2, waiting for transfers between devices, layer_backward(): lax.psum(partial_in, 'tensor') + times_transposed(grad_bc_low, w_bc)  72.5 us
  transfers between devices with their start and end apart: 22, of which 11 were waited for; matrix products, arithmetic and copies ran while one was open for 25% of the time, Pallas kernels for 0%

commit v1 on v0

v1 whole, which is shorter than its diff:
```python
import functools
import types

import jax
import jax.numpy as jnp
from jax import lax
from jax.experimental import pallas as pl
from jax.experimental.pallas import tpu as pltpu
from jax.sharding import PartitionSpec as P

f32, bf16 = jnp.float32, jnp.bfloat16
EPS = 1e-05
CONV = 4
HD = 64
MESH = pl.DeviceIdType.MESH
RB = 64


def nn(a, b):
    return lax.dot_general(a, b, (((1,), (0,)), ((), ())), preferred_element_type=f32)


def nt(a, b):
    return lax.dot_general(a, b, (((1,), (1,)), ((), ())), preferred_element_type=f32)


def tn(a, b):
    return lax.dot_general(a, b, (((0,), (0,)), ((), ())), preferred_element_type=f32)


def iota(shape, axis):
    return lax.broadcasted_iota(jnp.int32, shape, axis)


def ones_where(condition, dtype=bf16):
    return jnp.where(condition, 1.0, 0.0).astype(dtype)


def sigmoid(v):
    return 1.0 / (1.0 + jnp.exp(-v))


def parts3(x):
    high = x.astype(bf16).astype(f32)
    rest = x - high
    middle = rest.astype(bf16).astype(f32)
    return [high, middle, rest - middle]


def columns_of(rows_list):
    parts = [p for x in rows_list for p in parts3(x)]
    length = rows_list[0].shape[1]
    parts.append(jnp.zeros((128 - 8 * len(parts), length), f32))
    return jnp.concatenate(parts, axis=0).T.astype(bf16)


def pick(which, width, row_of_lane):
    r, lane = iota((128, width), 0), iota((128, width), 1)
    mine = (r >= 24 * which) & (r < 24 * which + 24)
    return ones_where(mine & ((r & 7) == row_of_lane(lane)))


def over(total, block, body):
    def step(i, carry):
        body(pl.ds(pl.multiple_of(i * block, block), block), i)
        return carry

    lax.fori_loop(0, total // block, step, 0)


class Op:
    def __init__(self, k, send, recv, sent, received, when_send=None, when_recv=None):
        self.send, self.recv = k.send_sems.at[send], k.recv_sems.at[recv]
        self.sent, self.received = sent, received
        self.when_send, self.when_recv = when_send, when_recv

    def to(self, src, dst, **device):
        pltpu.make_async_remote_copy(
            src_ref=src,
            dst_ref=dst,
            send_sem=self.send,
            recv_sem=self.recv,
            device_id=device,
            device_id_type=MESH,
        ).start()

    def arrived(self):
        def wait():
            pltpu.make_async_copy(self.received, self.received, self.recv).wait()

        wait() if self.when_recv is None else pl.when(self.when_recv)(wait)

    def left(self):
        def wait():
            pltpu.make_async_copy(self.sent, self.sent, self.send).wait()

        wait() if self.when_send is None else pl.when(self.when_send)(wait)


def scratch_of(T, D, NC, S, TP, DP):
    TB = T // TP
    G2 = 2 * S
    v = pltpu.VMEM
    return dict(
        hb=v((2, T, D), bf16),
        n2=v((2, 2 * T, D), bf16),
        go2=v((2, 2 * T, D), bf16),
        wz=v((2, D, NC), bf16),
        wx=v((2, D, NC), bf16),
        wbc=v((2, D, G2), bf16),
        wdt=v((2, 128, D), bf16),
        wout=v((2, NC, D), bf16),
        pk=v((2, 16, D), f32),
        pkown=v((16, D), f32),
        cmask=v((3, T + 8, G2), f32),
        madd=v((T, T), f32),
        pmask=v((T, NC), f32),
        tmask=v((T, NC), f32),
        tri=v((T, T), bf16),
        xe=v((2, T + 8, NC), f32),
        be=v((2, T + 8, G2), f32),
        gate=v((2, T, NC), f32),
        va=v((2, T, NC), f32),
        vb=v((2, T, G2), f32),
        X=v((2, T, NC), f32),
        Bm=v((2, T, S), bf16),
        Cm=v((2, T, S), bf16),
        xt=v((2, T, NC), bf16),
        xtail=v((2, T, NC), bf16),
        blk=v((3 * T, NC), bf16),
        M=v((2, 3, T, T), f32),
        G=v((2, T, T), f32),
        Wc=v((2, T, 3 * T), bf16),
        ccs=v((T, 3 * T), f32),
        dte=v((2, T, NC), f32),
        cex=v((T, NC), f32),
        ee=v((2, T, NC), f32),
        tl=v((2, T, NC), f32),
        stp=v((2, 8, T), f32),
        arow=v((2, 8, T), f32),
        sgd=v((2, 8, T), f32),
        yv=v((T, NC), f32),
        yin=v((2, T, NC), f32),
        mx=v((2, T, NC), f32),
        gd=v((2, T, NC), f32),
        gg=v((2, T, NC), bf16),
        sq=v((T, NC), bf16),
        sq2=v((T, NC), bf16),
        gni=v((T, NC), f32),
        s0=v((2, S, NC), f32),
        stS=v((4, S + 16, 256), bf16),
        stR=v((4, DP - 1, S + 16, 256), bf16),
        arS=v((2, 8, T), f32),
        arR=v((2, TP - 1, 8, T), f32),
        us=v((4, T, D), bf16),
        ur=v((4, TP - 1, TB, D), bf16),
        own=v((4, TB, D), bf16),
        u0=v((TB, D), f32),
        rex=v((2, T, NC), f32),
        kex=v((T, NC), f32),
        crossS=v((TB, 256), f32),
        cross=v((T, 256), f32),
        gm=v((T, NC), f32),
        eg=v((T, NC), bf16),
        gz2=v((2, 2 * T, NC), bf16),
        gx2=v((2, 2 * T, NC), bf16),
        ni2=v((2, 2 * T, NC), bf16),
        gdt2=v((2, 8, 2 * T), f32),
        dxt=v((T, NC), f32),
        dW=v((3, T, T), f32),
        Pb=v((3, T, T), bf16),
        dG=v((T, T), bf16),
        bes=v((T, NC), f32),
        qs=v((T, NC), bf16),
        gis=v((T, NC), bf16),
        dds=v((T, NC), bf16),
        dbc=v((T, G2), f32),
        ux=v((2, T + 8, NC), f32),
        ub=v((2, T + 8, G2), f32),
        gbp=v((2, T, G2), bf16),
        gbr=v((2, TP - 1, TB, G2), bf16),
        gbo=v((2, TB, G2), bf16),
        gb2=v((2, 2 * T, G2), bf16),
        nT=v((D, 2 * T), bf16),
        dzS=v((2, D, NC), bf16),
        dzR=v((2, DP - 1, D // DP, NC), bf16),
        dzO=v((2, D // DP, NC), bf16),
        dxS=v((2, D, NC), bf16),
        dxR=v((2, DP - 1, D // DP, NC), bf16),
        dxO=v((2, D // DP, NC), bf16),
        doS=v((2, NC, D), bf16),
        doR=v((2, DP - 1, NC // DP, D), bf16),
        doO=v((2, NC // DP, D), bf16),
        dbS=v((2, D // TP, G2), bf16),
        dbR=v((2, DP - 1, D // TP, G2), bf16),
        dbO=v((2, D // TP, G2), bf16),
        dtS=v((2, 8, D), f32),
        dtR=v((2, DP - 1, 8, D), f32),
        gpS=v((2, 8, 384), f32),
        gpR=v((2, TP - 1, 8, 384), f32),
        fpS=v((2, 24, 384), f32),
        fpR=v((2, 2 * DP - 1, 24, 384), f32),
        w_sems=pltpu.SemaphoreType.DMA((6, 2)),
        l_sems=pltpu.SemaphoreType.DMA((24,)),
        send_sems=pltpu.SemaphoreType.DMA((96,)),
        recv_sems=pltpu.SemaphoreType.DMA((96,)),
    )


INPUTS = (
    "i_tokens",
    "i_cot",
    "i_wz",
    "i_wx",
    "i_wbc",
    "i_wdt",
    "i_wout",
    "i_pre",
    "i_cx",
    "i_cbc",
    "i_bx",
    "i_bbc",
    "i_gain",
    "i_seq",
    "i_dtb",
    "i_alog",
    "i_dsk",
)
OUTPUTS = ("o_sec", "o_ing", "o_wz", "o_wx", "o_wbc", "o_wout", "o_dt", "o_pack")


def kernel(geo, names, *refs):
    k = types.SimpleNamespace(**dict(zip(names, refs)))
    T, D, NC, S, TP, DP = geo
    TB, G2, INNER = T // TP, 2 * S, NC * TP
    c, d, t = lax.axis_index("pipe"), lax.axis_index("dp"), lax.axis_index("tensor")
    other = 1 - c
    mine = pl.ds(pl.multiple_of(t * TB, TB), TB)
    ids = iter(range(96))
    pending = []

    def op(sent, received, when_send=None, when_recv=None):
        i = next(ids)
        made = Op(k, i, i, sent, received, when_send, when_recv)
        pending.append(made)
        return made

    def local(src, dst, i):
        return pltpu.make_async_copy(src, dst, k.l_sems.at[i])

    def peers(body, first=1):
        def step(j, carry):
            body(j, lax.rem(t + j, TP))
            return carry

        lax.fori_loop(first, TP, step, 0)

    in_tokens = local(k.i_tokens.at[c], k.hb.at[0], 0)
    in_tokens.start()
    weights = [("wx", 0), ("wbc", 1), ("wdt", 2), ("wz", 3), ("wout", 4)]

    def held(name):
        ref = getattr(k, name)
        return ref.at[c, 0:16] if name == "wdt" else ref.at[c]

    for name, i in weights:
        pltpu.make_async_copy(getattr(k, "i_" + name).at[0], held(name), k.w_sems.at[i, c]).start()
    in_cot = local(k.i_cot.at[c], k.go2.at[1, 0:T], 1)
    in_cot.start()
    in_cot_other = local(k.i_cot.at[other], k.go2.at[1, T : 2 * T], 2)
    in_cot_other.start()

    pk = k.pkown
    pk[...] = jnp.zeros_like(pk)
    pk[0:1, :] = k.i_pre[...]
    pk[1:5, 0:NC] = k.i_cx[0]
    pk[1:5, 256 : 256 + G2] = k.i_cbc[0]
    pk[5:6, 0:NC] = k.i_bx[...]
    pk[5:6, 256 : 256 + G2] = k.i_bbc[...]
    pk[6:7, 0:NC] = k.i_gain[...]
    head = iota((1, NC), 1) // HD
    skip = jnp.zeros((1, NC), f32)
    for h in range(3):
        pk[8 + h : 9 + h, 0:T] = jnp.full((1, T), k.i_dtb[0, h], f32)
        pk[8 + h : 9 + h, T : 2 * T] = jnp.full((1, T), k.i_alog[0, h], f32)
        skip = jnp.where(head == h, k.i_dsk[0, h], skip)
    pk[7:8, 0:NC] = skip
    pltpu.make_async_copy(k.pkown, k.pk.at[c], k.w_sems.at[5, c]).start()

    barrier = pltpu.get_barrier_semaphore()

    def greet(**device):
        pl.semaphore_signal(barrier, inc=1, device_id=device, device_id_type=MESH)

    peers(lambda j, to: greet(tensor=to))
    peers(lambda j, to: greet(pipe=other, tensor=to), 0)
    for j in range(1, DP):
        greet(dp=lax.rem(d + j, DP))
        greet(pipe=other, dp=lax.rem(d + j, DP))
    pl.semaphore_wait(barrier, 2 * TP - 1 + 2 * (DP - 1))

    w_sent = []

    def give(src, dst, i):
        send = k.send_sems.at[next(ids)]
        copy = pltpu.make_async_remote_copy(
            src_ref=src,
            dst_ref=dst,
            send_sem=send,
            recv_sem=k.w_sems.at[i, c],
            device_id={"pipe": other},
            device_id_type=MESH,
        )
        copy.start()
        w_sent.append(copy)

    give(k.pkown, k.pk.at[c], 5)
    for name, i in weights:
        give(getattr(k, "i_" + name).at[0], held(name), i)

    def have(name, i, l):
        ref = getattr(k, name)
        ref = ref.at[l, 0:16] if name == "wdt" else ref.at[l]
        pltpu.make_async_copy(ref, ref, k.w_sems.at[i, l]).wait()

    first_end = k.i_seq[c, 0]
    second_end = first_end + k.i_seq[c, 1]

    def seq_id(p):
        counted = jnp.where(p >= first_end, 1, 0) + jnp.where(p >= second_end, 1, 0)
        return jnp.where(p < 0, -1, counted)

    start = d * T
    for lag in range(1, CONV):
        p = start + iota((T + 8, G2), 0)
        k.cmask[lag - 1] = ones_where(seq_id(p) == seq_id(p - lag), f32)
    p_row, p_col = start + iota((T, T), 0), start + iota((T, T), 1)
    k.madd[...] = jnp.where((seq_id(p_row) == seq_id(p_col)) & (p_row >= p_col), 0.0, -1e30)
    k.tri[...] = ones_where(p_row <= p_col)
    p_row = start + iota((T, NC), 0)
    id_row = seq_id(p_row)
    k.pmask[...] = ones_where(id_row == seq_id(p_row * 0 + (start - 1)), f32)
    k.tmask[...] = ones_where(id_row == seq_id(p_row * 0 + (start + T - 1)), f32)
    for l in range(2):
        k.wdt[l, 16:128, :] = jnp.zeros((112, D), bf16)

    def running(x, backward=False):
        p = jnp.concatenate(parts3(x) + [jnp.zeros_like(x)], axis=0).astype(bf16)
        y = nt(p, k.tri[...]) if backward else nn(p, k.tri[...])
        return y[0:8] + y[8:16] + y[16:24]

    def heads_of(lane):
        return lane // HD

    per_head = ones_where(iota((8, NC), 0) == iota((8, NC), 1) // HD)

    def joined(slot, have_k):
        total, through = jnp.zeros((S, NC), f32), jnp.ones((1, NC), f32)
        for j in range(1, DP):
            part = k.stR[slot, j - 1, 0:S, 0:NC].astype(f32)
            decay = k.stR[slot, j - 1, S : S + 16, 0:NC].astype(f32)[0:1]
            total = total + (through * have_k(j)) * part
            through = through * decay
        return total

    def scatter(slot):
        made = op(k.ur.at[slot], k.ur.at[slot])

        def body(j, to):
            rows = pl.ds(pl.multiple_of(to * TB, TB), TB)
            made.to(k.us.at[slot, rows], k.ur.at[slot, j - 1], tensor=to)

        peers(body)
        return made

    def summed(made, slot):
        made.arrived()
        total = k.us[slot, mine, :].astype(f32)
        for j in range(TP - 1):
            total = total + k.ur[slot, j].astype(f32)
        return total

    def forward(l):
        have("pk", 5, l)

        def norm(r, i):
            h = k.hb[l, r, :].astype(f32)
            scale = lax.rsqrt(jnp.mean(h * h, axis=1, keepdims=True) + EPS)
            k.n2[l, r, :] = (h * scale * k.pk[l, 0:1, :]).astype(bf16)

        over(T, 32, norm)
        send_n = op(k.n2.at[l, 0:T], k.n2.at[l, T : 2 * T], c != l, c == l)
        pl.when(c != l)(
            lambda: send_n.to(k.n2.at[l, 0:T], k.n2.at[l, T : 2 * T], pipe=other)
        )
        have("wx", 0, l)
        k.xe[l, 8 : 8 + T, :] = nn(k.n2[l, 0:T, :], k.wx[l])
        have("wbc", 1, l)
        k.be[l, 8 : 8 + T, :] = nn(k.n2[l, 0:T, :], k.wbc[l])
        halo_x = op(k.xe.at[l, T : T + 8], k.xe.at[l, 0:8])
        halo_b = op(k.be.at[l, T : T + 8], k.be.at[l, 0:8])
        after = lax.rem(d + 1, DP)
        halo_x.to(k.xe.at[l, T : T + 8], k.xe.at[l, 0:8], dp=after)
        halo_b.to(k.be.at[l, T : T + 8], k.be.at[l, 0:8], dp=after)
        have("wdt", 2, l)
        dtp = nt(k.wdt[l, 0:16, :], k.n2[l, 0:T, :])[0:8] + k.pk[l, 8:16, 0:T]
        step = jnp.maximum(dtp, 0.0) + jnp.log1p(jnp.exp(-jnp.abs(dtp)))
        a = -jnp.exp(k.pk[l, 8:16, T : 2 * T]) * step
        run = running(a)
        k.stp[l], k.arow[l], k.sgd[l] = step, a, sigmoid(dtp)
        have("wz", 3, l)
        k.gate[l] = nn(k.n2[l, 0:T, :], k.wz[l])
        cols = columns_of([run, step])
        k.cex[...] = nn(cols, pick(0, NC, heads_of))
        k.dte[l] = nn(cols, pick(1, NC, heads_of))
        k.ccs[...] = nn(cols, pick(0, 3 * T, lambda lane: lane // T))

        def decays(r, i):
            here = k.cex[r, :]
            k.ee[l, r, :] = jnp.exp(here) * k.pmask[r, :]
            k.tl[l, r, :] = jnp.exp(k.cex[T - 1 : T, :] - here) * k.tmask[r, :]

        over(T, RB, decays)
        halo_x.arrived()
        halo_b.arrived()

        def conv(r, i):
            near = pl.ds(pl.multiple_of(i * RB, RB), RB + 8)
            for ext, lane, width in ((k.xe, 0, NC), (k.be, 256, G2)):
                block = ext[l, near, :]
                lanes = slice(lane, lane + width)
                v = k.pk[l, 5:6, lanes] + k.pk[l, 4:5, lanes] * block[8:]
                for lag in range(1, CONV):
                    moved = block[8 - lag : RB + 8 - lag] * k.cmask[lag - 1, r, 0:width]
                    v = v + k.pk[l, 4 - lag : 5 - lag, lanes] * moved
                act = v * sigmoid(v)
                if lane == 0:
                    k.va[l, r, :] = v
                    k.X[l, r, :] = act
                    xt = act * k.dte[l, r, :]
                    k.xt[l, r, :] = xt.astype(bf16)
                    k.xtail[l, r, :] = (xt * k.tl[l, r, :]).astype(bf16)
                    for h in range(3):
                        at = pl.ds(pl.multiple_of(h * T + i * RB, RB), RB)
                        k.blk[at, :] = jnp.where(head == h, xt, 0.0).astype(bf16)
                else:
                    k.vb[l, r, :] = v
                    k.Bm[l, r, :] = act[:, 0:S].astype(bf16)
                    k.Cm[l, r, :] = act[:, S:G2].astype(bf16)

        over(T, RB, conv)
        k.stS[l, 0:S, 0:NC] = tn(k.Bm[l], k.xtail[l]).astype(bf16)
        k.stS[l, S : S + 16, 0:NC] = jnp.broadcast_to(k.ee[l, T - 1 : T, :], (16, NC)).astype(bf16)
        states = op(k.stR.at[l], k.stR.at[l])
        for j in range(1, DP):
            states.to(k.stS.at[l], k.stR.at[l, j - 1], dp=lax.rem(d + j, DP))
        k.G[l] = nt(k.Cm[l], k.Bm[l])

        def mixing(r, i):
            for h in range(3):
                lanes = slice(h * T, h * T + T)
                m = jnp.exp(k.ccs[r, lanes] - run[h : h + 1, :] + k.madd[r, :])
                k.M[l, h, r, :] = m
                k.Wc[l, r, lanes] = (k.G[l, r, :] * m).astype(bf16)

        over(T, 32, mixing)
        k.yv[...] = nn(k.Wc[l], k.blk[...])
        if l == 1:
            have("wout", 4, l)
            k.gni[...] = nt(k.go2[1, 0:T, :], k.wout[1])
        states.arrived()
        k.s0[l] = joined(l, lambda j: jnp.where(d >= j, 1.0, 0.0))
        k.yin[l] = nn(k.Cm[l], k.s0[l].astype(bf16)) * k.ee[l]

        def gating(r, i):
            z = k.gate[l, r, :]
            mixed = k.yv[r, :] + k.yin[l, r, :] + k.pk[l, 7:8, 0:NC] * k.X[l, r, :]
            gated = mixed * z * sigmoid(z)
            k.mx[l, r, :] = mixed
            k.gd[l, r, :] = gated
            scaled = gated * k.pk[l, 6:7, 0:NC]
            k.gg[l, r, :] = scaled.astype(bf16)
            k.sq[r, :] = (gated * gated).astype(bf16)
            if l == 1:
                k.sq2[r, :] = (scaled * k.gni[r, :]).astype(bf16)

        over(T, RB, gating)
        row = iota((8, NC), 0)
        sums = nt(ones_where(row == 0), k.sq[...])
        if l == 1:
            sums = sums + nt(ones_where(row == 1), k.sq2[...])
        k.arS[l] = sums
        small = op(k.arR.at[l], k.arR.at[l])
        peers(lambda j, to: small.to(k.arS.at[l], k.arR.at[l, j - 1], tensor=to))
        if l == 0:
            have("wout", 4, l)
        for j in range(D // 256):
            lanes = slice(256 * j, 256 * j + 256)
            k.us[l, :, lanes] = nn(k.gg[l], k.wout[l, :, lanes]).astype(bf16)
        made = scatter(l)
        small.arrived()
        total = k.arS[l]
        for j in range(TP - 1):
            total = total + k.arR[l, j]
        r = lax.rsqrt(total[0:1] / INNER + EPS)
        factor = r * r * r * (total[1:2] / INNER)
        cols = columns_of([jnp.concatenate([r, factor, jnp.zeros((6, T), f32)], axis=0)])
        k.rex[l] = nn(cols, pick(0, NC, lambda lane: 0 * lane))
        if l == 1:
            k.kex[...] = nn(cols, pick(0, NC, lambda lane: 0 * lane + 1))
        return made, send_n

    def section_rows(l, made):
        total = summed(made, l)
        if l == 0:
            k.u0[...] = total
        out = k.hb[l, mine, :].astype(f32) + k.rex[l, mine, 0:1] * total
        k.own[l] = out.astype(bf16)

    def spread_out(slot, out, l):
        near = op(out.at[0, 0, 0 : T - TB], out.at[0, 0, 0 : T - TB], c == l, c == l)
        far = op(out.at[0, 0, 0:T], out.at[0, 0, 0:T], c != l, c == l)
        dst = out.at[0, c, mine]
        keep = local(k.own.at[slot], dst, 8 + slot)

        @pl.when(c == l)
        def _():
            peers(lambda j, to: near.to(k.own.at[slot], dst, tensor=to))
            keep.start()

        @pl.when(c != l)
        def _():
            peers(lambda j, to: far.to(k.own.at[slot], dst, pipe=other, tensor=to), 0)

        return near, far, lambda: pl.when(c == l)(keep.wait)

    def gather_in(slot, buffer):
        made = op(buffer.at[0 : T - TB], buffer.at[0 : T - TB])
        dst = buffer.at[mine]
        peers(lambda j, to: made.to(k.own.at[slot], dst, tensor=to))
        dst[...] = k.own[slot]
        return made

    def hand_out(src, out, l, i):
        far = op(src, out.at[0, 0], c != l, c == l)
        keep = local(src, out.at[0, c], i)

        @pl.when(c == l)
        def _():
            keep.start()

        @pl.when(c != l)
        def _():
            far.to(src, out.at[0, c], pipe=other)

        return far, lambda: pl.when(c == l)(keep.wait)

    def backward(l):
        if l == 0:
            k.gni[...] = nt(k.go2[0, 0:T, :], k.wout[0])

        def gates(r, i, sums):
            z = k.gate[l, r, :]
            s = sigmoid(z)
            gn, gated, rx = k.gni[r, :], k.gd[l, r, :], k.rex[l, r, :]
            if l == 1:
                factor = k.kex[r, :]
            else:
                factor = rx * rx * rx * (k.cross[r, 0:NC] / INNER)
            gain = k.pk[l, 6:7, 0:NC]
            g = rx * (gn * gain) - gated * factor
            gm = g * z * s
            gz = g * k.mx[l, r, :] * s * (1.0 + z * (1.0 - s))
            k.gm[r, :] = gm
            k.gz2[l, r, :] = gz.astype(bf16)
            k.eg[r, :] = (gm * k.ee[l, r, :]).astype(bf16)
            k.ni2[l, r, :] = (gated * gain * rx).astype(bf16)
            for h in range(3):
                at = pl.ds(pl.multiple_of(h * T + i * RB, RB), RB)
                k.blk[at, :] = jnp.where(head == h, gm, 0.0).astype(bf16)
            by_gain = jnp.sum(gn * gated * rx, axis=0, keepdims=True)
            by_skip = jnp.sum(gm * k.X[l, r, :], axis=0, keepdims=True)
            return sums[0] + by_gain, sums[1] + by_skip

        zero = jnp.zeros((1, NC), f32)
        by_gain, by_skip = lax.fori_loop(
            0,
            T // RB,
            lambda i, s: gates(pl.ds(pl.multiple_of(i * RB, RB), RB), i, s),
            (zero, zero),
        )
        k.fpS[l] = jnp.zeros((24, 384), f32)
        k.fpS[l, 13:14, 0:NC] = by_gain
        k.fpS[l, 14:15, 0:NC] = by_skip
        k.stS[2 + l, 0:S, 0:NC] = tn(k.Cm[l], k.eg[...]).astype(bf16)
        k.stS[2 + l, S : S + 16, 0:NC] = k.stS[l, S : S + 16, 0:NC]
        states = op(k.stR.at[2 + l], k.stR.at[2 + l])
        for j in range(1, DP):
            states.to(k.stS.at[2 + l], k.stR.at[2 + l, j - 1], dp=lax.rem(d + DP - j, DP))
        dxt = jnp.zeros((T, NC), f32)
        for h in range(3):
            part = k.blk[h * T : h * T + T, :]
            dxt = dxt + tn(k.Wc[l, :, h * T : h * T + T], part)
            k.dW[h] = nt(part, k.xt[l])
        k.dxt[...] = dxt

        def pairs(r, i):
            g_sum = jnp.zeros((32, T), f32)
            for h in range(3):
                w = k.dW[h, r, :] * k.M[l, h, r, :]
                g_sum = g_sum + w
                k.Pb[h, r, :] = (w * k.G[l, r, :]).astype(bf16)
            k.dG[r, :] = g_sum.astype(bf16)

        over(T, 32, pairs)
        flow = jnp.zeros((8, T), f32)
        for h in range(3):
            one = ones_where(iota((8, T), 0) == h)
            flow = flow + nt(one, k.Pb[h]) - nn(one, k.Pb[h])
        states.arrived()
        after = joined(2 + l, lambda j: jnp.where(d + j < DP, 1.0, 0.0))
        through = jnp.sum(after * k.s0[l], axis=0, keepdims=True) * k.ee[l, T - 1 : T, :]
        constant = jnp.sum(per_head.astype(f32) * through, axis=1, keepdims=True)
        after = after.astype(bf16)
        k.bes[...] = nn(k.Bm[l], after)
        k.dbc[:, 0:S] = tn(k.dG[...], k.Cm[l]) + nt(k.xtail[l], after)
        k.dbc[:, S:G2] = nn(k.dG[...], k.Bm[l]) + nt(k.eg[...], k.s0[l].astype(bf16))

        def inputs(r, i):
            x, gm, dte = k.X[l, r, :], k.gm[r, :], k.dte[l, r, :]
            tail = k.tl[l, r, :] * k.bes[r, :]
            dx = k.dxt[r, :] + tail
            k.qs[r, :] = (x * dte * tail).astype(bf16)
            k.gis[r, :] = (gm * k.yin[l, r, :]).astype(bf16)
            k.dds[r, :] = (dx * x).astype(bf16)
            v = k.va[l, r, :]
            s = sigmoid(v)
            k.ux[l, r, :] = (dte * dx + k.pk[l, 7:8, 0:NC] * gm) * (s * (1.0 + v * (1.0 - s)))
            v = k.vb[l, r, :]
            s = sigmoid(v)
            k.ub[l, r, :] = k.dbc[r, :] * (s * (1.0 + v * (1.0 - s)))

        over(T, RB, inputs)
        halo_x = op(k.ux.at[l, 0:8], k.ux.at[l, T : T + 8])
        halo_b = op(k.ub.at[l, 0:8], k.ub.at[l, T : T + 8])
        before = lax.rem(d + DP - 1, DP)
        halo_x.to(k.ux.at[l, 0:8], k.ux.at[l, T : T + 8], dp=before)
        halo_b.to(k.ub.at[l, 0:8], k.ub.at[l, T : T + 8], dp=before)
        q, inter = nt(per_head, k.qs[...]), nt(per_head, k.gis[...])
        direct = nt(per_head, k.dds[...])
        da = running(flow + inter, True) + (running(q) - q) + constant
        a_log = k.pk[l, 8:16, T : 2 * T]
        gdt = (direct - jnp.exp(a_log) * da) * k.sgd[l]
        k.gdt2[l, :, 0:T] = gdt
        k.fpS[l, 16:24, 0:128] = jnp.broadcast_to(jnp.sum(gdt, axis=1, keepdims=True), (8, 128))
        by_a = jnp.sum(k.arow[l] * da, axis=1, keepdims=True)
        k.fpS[l, 16:24, 128:256] = jnp.broadcast_to(by_a, (8, 128))
        halo_x.arrived()
        halo_b.arrived()

        def conv_back(u, ext, lane, width, dst):
            lanes = slice(lane, lane + width)

            def step(i, sums):
                near = pl.ds(pl.multiple_of(i * RB, RB), RB + 8)
                r = pl.ds(pl.multiple_of(i * RB, RB), RB)
                ublock, before = u[l, near, :], ext[l, near, :]
                g = k.pk[l, 4:5, lanes] * ublock[0:RB]
                here = ublock[0:RB]
                out = [
                    sums[0] + jnp.sum(here * before[8:], axis=0, keepdims=True),
                ]
                for lag in range(1, CONV):
                    masked = ublock * k.cmask[lag - 1, near, 0:width]
                    g = g + k.pk[l, 4 - lag : 5 - lag, lanes] * masked[lag : RB + lag]
                    moved = before[8 - lag : RB + 8 - lag]
                    out.append(
                        sums[lag] + jnp.sum(masked[0:RB] * moved, axis=0, keepdims=True)
                    )
                out.append(sums[CONV] + jnp.sum(here, axis=0, keepdims=True))
                dst[l, r, :] = g.astype(bf16)
                return tuple(out)

            zero = jnp.zeros((1, width), f32)
            return lax.fori_loop(0, T // RB, step, (zero,) * (CONV + 1))

        by_bc = conv_back(k.ub, k.be, 256, G2, k.gbp)
        bc = op(k.gbr.at[l], k.gbr.at[l])

        def give_bc(j, to):
            rows = pl.ds(pl.multiple_of(to * TB, TB), TB)
            bc.to(k.gbp.at[l, rows], k.gbr.at[l, j - 1], tensor=to)

        peers(give_bc)
        by_x = conv_back(k.ux, k.xe, 0, NC, k.gx2)
        k.gpS[l] = jnp.zeros((8, 384), f32)
        for lag in range(CONV):
            k.fpS[l, 8 + 3 - lag : 9 + 3 - lag, 0:NC] = by_x[lag]
            k.gpS[l, 4 + 3 - lag : 5 + 3 - lag, 0:G2] = by_bc[lag]
        k.fpS[l, 12:13, 0:NC] = by_x[CONV]
        k.gpS[l, 4:5, G2 : G2 + 128] = by_bc[CONV][:, 0:128]
        k.gpS[l, 5:6, G2 : G2 + 128] = by_bc[CONV][:, 128:256]
        gdt_cols = jnp.concatenate([gdt, jnp.zeros((120, T), f32)], axis=0).T.astype(bf16)
        for j in range(D // 256):
            at = slice(256 * j, 256 * j + 256)
            part = nt(k.gz2[l, 0:T, :], k.wz[l, at, :]) + nt(k.gx2[l, 0:T, :], k.wx[l, at, :])
            part = part + nt(k.gbp[l], k.wbc[l, at, :]) + nn(gdt_cols, k.wdt[l, :, at])
            k.us[2 + l, :, at] = part.astype(bf16)
        return scatter(2 + l), bc

    def input_rows(l, made):
        gn = summed(made, 2 + l)
        h = k.hb[l, mine, :].astype(f32)
        scale = lax.rsqrt(jnp.mean(h * h, axis=1, keepdims=True) + EPS)
        weighted = gn * k.pk[l, 0:1, :]
        inner = jnp.sum(weighted * h, axis=1, keepdims=True)
        gh = scale * weighted - h * (scale * scale * scale * (1.0 / D) * inner)
        low = (k.go2[l, mine, :].astype(f32) + gh).astype(bf16)
        k.own[2 + l] = low
        by_pre = jnp.sum(gn * h * scale, axis=0, keepdims=True)
        for j in range(4):
            k.gpS[l, j : j + 1, :] = by_pre[:, 384 * j : 384 * j + 384]
        if l == 1:
            sums = jnp.sum(low.astype(f32) * k.u0[...], axis=1, keepdims=True)
            k.crossS[...] = jnp.broadcast_to(sums, (TB, 256))

    def operands(l):
        pairs = [(k.gz2.at[l, 0:T], k.gz2.at[l, T : 2 * T])]
        pairs += [(k.gx2.at[l, 0:T], k.gx2.at[l, T : 2 * T])]
        pairs += [(k.ni2.at[l, 0:T], k.ni2.at[l, T : 2 * T])]
        pairs += [(k.gdt2.at[l, :, 0:T], k.gdt2.at[l, :, T : 2 * T])]
        ops = [op(a, b, c != l, c == l) for a, b in pairs]

        @pl.when(c != l)
        def _():
            for made, (a, b) in zip(ops, pairs):
                made.to(a, b, pipe=other)

        return ops

    def bc_total(l, bc):
        bc.arrived()
        total = k.gbp[l, mine, :].astype(f32)
        for j in range(TP - 1):
            total = total + k.gbr[l, j].astype(f32)
        k.gbo[l] = total.astype(bf16)
        near = op(k.gb2.at[l, 0 : T - TB], k.gb2.at[l, 0 : T - TB], c == l, c == l)
        far = op(k.gb2.at[l, 0:T], k.gb2.at[l, 0:T], c != l, c == l)

        @pl.when(c == l)
        def _():
            peers(lambda j, to: near.to(k.gbo.at[l], k.gb2.at[l, mine], tensor=to))
            k.gb2[l, mine, :] = k.gbo[l]

        @pl.when(c != l)
        def _():
            there = pl.ds(pl.multiple_of(T + t * TB, TB), TB)
            peers(
                lambda j, to: far.to(k.gbo.at[l], k.gb2.at[l, there], pipe=other, tensor=to),
                0,
            )

        return near, far

    def ring(l, name, axis_rows):
        sent, recv = getattr(k, name + "S"), getattr(k, name + "R")
        made = op(recv.at[l], recv.at[l], c == l, c == l)

        def start():
            for j in range(1, DP):
                to = lax.rem(d + j, DP)
                rows = pl.ds(pl.multiple_of(to * axis_rows, axis_rows), axis_rows)
                made.to(sent.at[l, rows], recv.at[l, j - 1], dp=to)

        return made, start

    def ring_end(l, name, made, out, axis_rows):
        sent, recv, own = (getattr(k, name + x) for x in "SRO")
        rows = pl.ds(pl.multiple_of(d * axis_rows, axis_rows), axis_rows)
        total_rows = axis_rows * (DP - 1)
        spread = op(out.at[0, 0:total_rows], out.at[0, 0:total_rows], c == l, c == l)

        def finish():
            made.arrived()
            total = sent[l, rows, :].astype(f32)
            for j in range(DP - 1):
                total = total + recv[l, j].astype(f32)
            own[l] = total.astype(bf16)
            for j in range(1, DP):
                spread.to(own.at[l], out.at[0, rows], dp=lax.rem(d + j, DP))

        return spread, finish, (own.at[l], out.at[0, rows])

    def weight_grads(l, n_op, factor_ops, bc_ops, go_op):
        dz, start_z = ring(l, "dz", D // DP)
        dx, start_x = ring(l, "dx", D // DP)
        do, start_o = ring(l, "do", NC // DP)
        dt_made = op(k.dtR.at[l], k.dtR.at[l], c == l, c == l)
        db_made = op(k.dbR.at[l], k.dbR.at[l], c == l, c == l)

        @pl.when(c == l)
        def _():
            pltpu.make_async_copy(n_op.received, n_op.received, n_op.recv).wait()
            for made in factor_ops:
                pltpu.make_async_copy(made.received, made.received, made.recv).wait()
            if go_op is not None:
                pltpu.make_async_copy(go_op.received, go_op.received, go_op.recv).wait()
            for j in range(D // 128):
                at = slice(128 * j, 128 * j + 128)
                k.nT[at, :] = k.n2[l, :, at].T
            k.dxS[l] = nn(k.nT[...], k.gx2[l]).astype(bf16)
            start_x()
            k.dzS[l] = nn(k.nT[...], k.gz2[l]).astype(bf16)
            start_z()
            for j in range(D // 256):
                at = slice(256 * j, 256 * j + 256)
                k.doS[l, :, at] = tn(k.ni2[l], k.go2[l, :, at]).astype(bf16)
            start_o()
            steps = jnp.concatenate([k.gdt2[l], jnp.zeros((8, 2 * T), f32)], axis=0).astype(bf16)
            k.dtS[l] = nn(steps, k.n2[l])[0:8]
            for j in range(1, DP):
                dt_made.to(k.dtS.at[l], k.dtR.at[l, j - 1], dp=lax.rem(d + j, DP))
            for made in bc_ops:
                pltpu.make_async_copy(made.received, made.received, made.recv).wait()
            part = pl.ds(pl.multiple_of(t * (D // TP), D // TP), D // TP)
            k.dbS[l] = nn(k.nT[part, :], k.gb2[l]).astype(bf16)
            for j in range(1, DP):
                db_made.to(k.dbS.at[l], k.dbR.at[l, j - 1], dp=lax.rem(d + j, DP))

        return dz, dx, do, dt_made, db_made

    def weight_ends(l, made):
        dz, dx, do, dt_made, db_made = made
        ends = [
            ring_end(l, "dx", dx, k.o_wx, D // DP),
            ring_end(l, "dz", dz, k.o_wz, D // DP),
            ring_end(l, "do", do, k.o_wout, NC // DP),
        ]
        slab = D // TP
        rows = pl.ds(pl.multiple_of(t * slab, slab), slab)
        count = slab * (TP - 1)
        spread = op(k.o_wbc.at[0, 0:count], k.o_wbc.at[0, 0:count], c == l, c == l)

        @pl.when(c == l)
        def _():
            copies = []
            for i, (_, finish, (src, dst)) in enumerate(ends):
                finish()
                copies.append(local(src, dst, 12 + i))
                copies[-1].start()
            db_made.arrived()
            total = k.dbS[l].astype(f32)
            for j in range(DP - 1):
                total = total + k.dbR[l, j].astype(f32)
            k.dbO[l] = total.astype(bf16)
            peers(lambda j, to: spread.to(k.dbO.at[l], k.o_wbc.at[0, rows], tensor=to))
            copies.append(local(k.dbO.at[l], k.o_wbc.at[0, rows], 15))
            copies[-1].start()
            dt_made.arrived()
            total = k.dtS[l]
            for j in range(DP - 1):
                total = total + k.dtR[l, j]
            k.o_dt[...] = total
            for copy in copies:
                copy.wait()

        return [e[0] for e in ends] + [spread]

    def small_start(l):
        made = op(k.gpR.at[l], k.gpR.at[l])
        peers(lambda j, to: made.to(k.gpS.at[l], k.gpR.at[l, j - 1], tensor=to))
        return made

    def small_middle(l, made):
        made.arrived()
        total = k.gpS[l]
        for j in range(TP - 1):
            total = total + k.gpR[l, j]
        k.fpS[l, 0:8, :] = total
        near = op(k.fpR.at[l, 0 : DP - 1], k.fpR.at[l, 0 : DP - 1], c == l, c == l)
        far = op(k.fpR.at[l, DP - 1 :], k.fpR.at[l, DP - 1 :], c != l, c == l)

        @pl.when(c == l)
        def _():
            for j in range(1, DP):
                near.to(k.fpS.at[l], k.fpR.at[l, j - 1], dp=lax.rem(d + j, DP))

        @pl.when(c != l)
        def _():
            for j in range(DP):
                far.to(k.fpS.at[l], k.fpR.at[l, DP - 1 + j], pipe=other, dp=lax.rem(d + j, DP))

        return near, far

    def small_end(l, made):
        for m in made:
            m.arrived()

        @pl.when(c == l)
        def _():
            total = k.fpS[l]
            for j in range(2 * DP - 1):
                total = total + k.fpR[l, j]
            k.o_pack[...] = total

    in_tokens.wait()
    made, n_op0 = forward(0)
    section_rows(0, made)
    gather = gather_in(0, k.hb.at[1])
    gather.arrived()
    sec0, sec0_keep = hand_out(k.hb.at[1], k.o_sec, 0, 3)
    in_cot.wait()
    in_cot_other.wait()
    made1, n_op1 = forward(1)
    made2, bc1 = backward(1)
    factors1 = operands(1)
    section_rows(1, made1)
    sec1 = spread_out(1, k.o_sec, 1)
    input_rows(1, made2)
    gather = gather_in(3, k.go2.at[0, 0:T])
    cross = op(k.cross.at[0 : T - TB], k.cross.at[0 : T - TB])
    peers(lambda j, to: cross.to(k.crossS, k.cross.at[mine], tensor=to))
    k.cross[mine, :] = k.crossS[...]
    small1 = small_start(1)
    bc_ops1 = bc_total(1, bc1)
    gather.arrived()
    cross.arrived()
    ing1, ing1_keep = hand_out(k.go2.at[0, 0:T], k.o_ing, 1, 4)
    go_op = op(k.go2.at[0, 0:T], k.go2.at[0, T : 2 * T], c != 0, c == 0)
    pl.when(c != 0)(
        lambda: go_op.to(k.go2.at[0, 0:T], k.go2.at[0, T : 2 * T], pipe=other)
    )
    grads1 = weight_grads(1, n_op1, factors1, bc_ops1, None)
    made3, bc0 = backward(0)
    factors0 = operands(0)
    bc_ops0 = bc_total(0, bc0)
    grads0 = weight_grads(0, n_op0, factors0, bc_ops0, go_op)
    packs1 = small_middle(1, small1)
    spreads = weight_ends(1, grads1)
    input_rows(0, made3)
    ing0 = spread_out(2, k.o_ing, 0)
    small0 = small_start(0)
    spreads += weight_ends(0, grads0)
    packs0 = small_middle(0, small0)
    small_end(1, packs1)
    small_end(0, packs0)
    sec0.arrived()
    sec0_keep()
    ing1.arrived()
    ing1_keep()
    for near, far, keep in (sec1, ing0):
        near.arrived()
        far.arrived()
        keep()
    for spread in spreads:
        spread.arrived()
    for copy in w_sent:
        copy.wait_send()
    for made in pending:
        made.left()


def on_device(sizes, *args):
    (tokens, seq, cot, pre, wz, wx, wbc, wdt, cx, cbc, bx, bbc, dtb, alog, dsk, gain, wout) = args
    TP, DP = sizes
    _, T, D = tokens.shape
    NC, S = wx.shape[2], wbc.shape[2] // 2
    wdt = jnp.pad(jnp.swapaxes(wdt, 1, 2), ((0, 0), (0, 13), (0, 0)))
    scratch = scratch_of(T, D, NC, S, TP, DP)
    names = tuple(INPUTS) + tuple(OUTPUTS) + tuple(scratch)
    any_, vmem, smem = (pl.BlockSpec(memory_space=m) for m in (pl.ANY, pltpu.VMEM, pltpu.SMEM))
    made = pl.pallas_call(
        functools.partial(kernel, (T, D, NC, S, TP, DP), names),
        out_shape=(
            jax.ShapeDtypeStruct((1, 2, T, D), bf16),
            jax.ShapeDtypeStruct((1, 2, T, D), bf16),
            jax.ShapeDtypeStruct((1, D, NC), bf16),
            jax.ShapeDtypeStruct((1, D, NC), bf16),
            jax.ShapeDtypeStruct((1, D, 2 * S), bf16),
            jax.ShapeDtypeStruct((1, NC, D), bf16),
            jax.ShapeDtypeStruct((8, D), f32),
            jax.ShapeDtypeStruct((24, 384), f32),
        ),
        in_specs=[any_] * 7 + [vmem] * 6 + [smem] * 4,
        out_specs=(any_,) * 6 + (vmem,) * 2,
        scratch_shapes=list(scratch.values()),
        compiler_params=pltpu.CompilerParams(
            collective_id=0, has_side_effects=True, vmem_limit_bytes=60 * 1024 * 1024
        ),
    )(tokens, cot, wz, wx, wbc, wdt, wout, pre, cx, cbc, bx, bbc, gain, seq, dtb, alog, dsk)
    sec, ing, dwz, dwx, dwbc, dwout, ddt, pack = made
    heads = NC // HD
    by_skip = pack[14, 0:NC].reshape(1, heads, HD).sum(axis=2)
    return (
        sec,
        ing,
        pack[0:4].reshape(1, D),
        dwz.astype(f32),
        dwx.astype(f32),
        dwbc.astype(f32),
        ddt[0:heads].T[None],
        pack[8:12, 0:NC][None],
        pack[4:8, 0 : 2 * S][None],
        pack[12:13, 0:NC],
        pack[4:6, 256:384].reshape(1, 2 * S),
        pack[16 : 16 + heads, 0][None],
        pack[16 : 16 + heads, 128][None],
        by_skip,
        pack[13:14, 0:NC],
        dwout.astype(f32),
    )


def solution(mesh):
    in_specs = (
        P(None, "dp", None),
        P(),
        P(None, "dp", None),
        P("pipe", None),
        P("pipe", None, "tensor"),
        P("pipe", None, "tensor"),
        P("pipe", None, None),
        P("pipe", None, "tensor"),
        P("pipe", None, "tensor"),
        P("pipe", None, None),
        P("pipe", "tensor"),
        P("pipe", None),
        P("pipe", "tensor"),
        P("pipe", "tensor"),
        P("pipe", "tensor"),
        P("pipe", "tensor"),
        P("pipe", "tensor", None),
    )
    out_specs = (
        P("pipe", None, "dp", None),
        P("pipe", None, "dp", None),
        P("pipe", None),
        P("pipe", None, "tensor"),
        P("pipe", None, "tensor"),
        P("pipe", None, None),
        P("pipe", None, "tensor"),
        P("pipe", None, "tensor"),
        P("pipe", None, None),
        P("pipe", "tensor"),
        P("pipe", None),
        P("pipe", "tensor"),
        P("pipe", "tensor"),
        P("pipe", "tensor"),
        P("pipe", "tensor"),
        P("pipe", "tensor", None),
    )
    return jax.shard_map(
        functools.partial(on_device, (mesh.shape["tensor"], mesh.shape["dp"])),
        mesh=mesh,
        in_specs=in_specs,
        out_specs=out_specs,
        check_vma=False,
    )
```

time: 2030 us -> 199 us (0.10); the launches traced: 2000 us -> 199 us
  waiting for transfers between devices: 571 us -> 0 us
  blocking collectives: 413 us -> 0 us
  local copies, waits for them, and re-layouts: 419 us -> 19.6 us
  other arithmetic: 287 us -> 3.03 us
  matrix products: 262 us -> 0 us
  Pallas kernels: 0 us -> 176 us
  starting transfers between devices: 31.3 us -> 0 us
    psum x9 -> x0, waiting for transfers between devices: 564 us -> none  [the longest x3 220 us: layer_forward(): total_out = lax.psum(partial_out, 'tensor')]
    dot_general x201 -> x0, matrix products: 262 us -> none  [the longest x30 51.9 us: group_scan(): jnp.einsum('hts,shp->thp', weights, head_block, precision=highest)]
    psum x6 -> x0, blocking collectives: 215 us -> none  [the longest x3 119 us: layer_forward(): square_sum = lax.psum(jnp.sum(gated_out * gated_out, axis=1), 'tensor')]
    all_gather x18 -> x0, blocking collectives: 198 us -> none  [carried_in(): pieces = jax.tree.map(lambda part: lax.all_gather(part, axis), value)]
    pallas_call x0 -> x1, Pallas kernels: none -> 176 us  [on_device(): pl.pallas_call(functools.partial(kernel, (T, D, NC, S, TP, DP), names), o...]
    dynamic_update_slice x30 -> x0, local copies, waits for them, and re-layouts: 83.4 us -> none  [ssd_parts(): lax.scan(jax.checkpoint(group_scan), zero_state, blocks)]
    another operation x64 -> x0, other arithmetic: 60.1 us -> none  [the longest x30 28.1 us: group_scan(): cumulative = jnp.cumsum(dt_block * rate_row[None, :], axis=0)]
    mul x107 -> x0, local copies, waits for them, and re-layouts: 56.2 us -> none  [the longest x27 19.6 us: link_states(): later[0][:, None, None] * earlier[1] + later[1]]
  transfers between devices with their start and end apart: 22 -> 0, of which waited for: 11 -> 0; matrix products, arithmetic and copies ran while one was open for 25% -> 0% of each run, Pallas kernels for 0% -> 0%
where the time goes in v1:
time: 199 us
  Pallas kernels  176 us (88%)
  local copies, waits for them, and re-layouts  19.6 us (10%)
  other arithmetic  3.03 us (2%)
    pallas_call x1, Pallas kernels, on_device(): pl.pallas_call(functools.partial(kernel, (T, D, NC, S, TP, DP), names), o...  176 us
    unnamed x25, local copies, waits for them, and re-layouts  12.3 us

profile of v1, /device:TPU:0, one launch (start us, length us, event | category | flops | bytes accessed | tf_op | source)
XLA Modules:
  0.0 199.0 jit_solution(7019557438492449873)
XLA Ops:
  0.6 0.0 copy-start.5
  0.7 0.0 copy-start.7
  0.7 2.3 %copy.38.refs_2_ = bf16[1,1536,192]{2,1,0:T(8,128)(2,1)} copy(bf16[1,1536,192]{1,2,0:T(8,128)(2,1)} %param.21) | data formatting | bytes 1179648 | tf_op args[4]
  2.9 0.0 copy-done.5
  2.9 1.2 copy.39.refs_3_
  4.1 0.0 copy-done.7
  4.1 0.6 pad.4.refs_5_
  4.7 175.6 %shard_map.288 = (bf16[1,2,256,1536]{3,2,1,0:T(8,128)(2,1)}, bf16[1,2,256,1536]{3,2,1,0:T(8,128)(2,1)}, bf16[1,1536,192]{2,1,0:T(8,128)(2,1)}, bf16[1,1536,192]{...) custom-call(bf16[2,256,1536]{2,1,0:T(8,128)(2,1)} %refs_0_.1, ...), custom_call_target="tpu_custom_call" | custom-call | tf_op jit(solution)/shard_map/pallas_call | solution.py:972
  180.4 0.0 copy-start.3
  180.4 0.8 slice_bitcast_fusion.1
  181.1 0.6 copy.43
  181.7 0.0 copy-start.2
  181.7 2.5 %copy.40 = f32[1,1536,192]{1,2,0:T(8,128)} copy(bf16[1,1536,192]{2,1,0:T(8,128)(2,1)} %get-tuple-element.27) | data formatting | bytes 1769472
  184.2 0.0 copy-done.3
  184.2 1.3 copy.41
  185.5 0.0 copy-start.6
  185.5 0.0 copy-start.4
  185.5 0.0 copy-done.2
  185.5 0.0 copy-start.1
  185.5 1.3 convert_element_type.16
  186.8 0.0 copy-done.6
  186.8 0.6 copy.42
  187.4 1.3 slice_bitcast_fusion.3
  188.7 1.3 slice_bitcast_fusion.2
  190.0 1.4 fusion
  191.4 1.2 slice.35
  192.6 1.3 slice_reduce_fusion
  194.0 0.1 reshape_squeeze.3
  194.1 0.6 reduce_sum.11
  194.7 0.0 copy-done.4
  194.7 1.1 convert_element_type.17
  195.8 0.0 copy-done.1
  195.8 0.0 copy-start
  195.8 1.1 copy.46
  197.0 0.8 copy-done
  197.8 1.1 copy.47
  (1 shorter events, 0.0 us)
Async XLA Ops:
  0.6 2.3 %copy-start.5 = (bf16[1,1536,192]{1,2,0:T(8,128)(2,1)S(1)}, bf16[1,1536,192]{1,2,0:T(8,128)(2,1)}, u32[]{:S(2)}) copy-start(bf16[1,1536,192]{1,2,0:T(8,128)(2,1)} %param.22) | copy-start | bytes 1769476
  0.7 3.4 %copy-start.7 = (bf16[1,1536,3]{1,2,0:T(4,128)(2,1)S(1)}, bf16[1,1536,3]{1,2,0:T(4,128)(2,1)}, u32[]{:S(2)}) copy-start(bf16[1,1536,3]{1,2,0:T(4,128)(2,1)} %param.24) | copy-start | bytes 27652
  180.4 3.9 %copy-start.3 = (bf16[1,1536,192]{2,1,0:T(8,128)(2,1)S(1)}, bf16[1,1536,192]{2,1,0:T(8,128)(2,1)}, u32[]{:S(2)}) copy-start(bf16[1,1536,192]{2,1,0:T(8,128)(2,1)} %get-tuple-element.28) | copy-start | bytes 1769476
  181.7 3.8 %copy-start.2 = (bf16[1,1536,256]{2,1,0:T(8,128)(2,1)S(1)}, bf16[1,1536,256]{2,1,0:T(8,128)(2,1)}, u32[]{:S(2)}) copy-start(bf16[1,1536,256]{2,1,0:T(8,128)(2,1)} %get-tuple-element.29) | copy-start | bytes 2359300
  185.5 1.3 copy-start.6
  185.5 9.2 %copy-start.4 = (bf16[1,192,1536]{2,1,0:T(8,128)(2,1)S(1)}, bf16[1,192,1536]{2,1,0:T(8,128)(2,1)}, u32[]{:S(2)}) copy-start(bf16[1,192,1536]{2,1,0:T(8,128)(2,1)} %get-tuple-element.31) | copy-start | bytes 1769476
  185.5 10.3 %copy-start.1 = (bf16[1,2,256,1536]{3,2,1,0:T(8,128)(2,1)S(1)}, bf16[1,2,256,1536]{3,2,1,0:T(8,128)(2,1)}, u32[]{:S(2)}) copy-start(bf16[1,2,256,1536]{3,2,1,0:T(8,128)(2,1)} %get-tuple-element.85) | copy-start | bytes 4718596
  195.8 2.0 copy-start

commit v2 on v1

--- a/solution.py
+++ b/solution.py
@@ -84,11 +84,16 @@
             device_id_type=MESH,
         ).start()
 
+    def beside(self, received, when_recv):
+        made = object.__new__(Op)
+        made.recv, made.received, made.when_recv = self.recv, received, when_recv
+        return made
+
+    def take(self):
+        pltpu.make_async_copy(self.received, self.received, self.recv).wait()
+
     def arrived(self):
-        def wait():
-            pltpu.make_async_copy(self.received, self.received, self.recv).wait()
-
-        wait() if self.when_recv is None else pl.when(self.when_recv)(wait)
+        self.take() if self.when_recv is None else pl.when(self.when_recv)(self.take)
 
     def left(self):
         def wait():
@@ -97,16 +102,17 @@
         wait() if self.when_send is None else pl.when(self.when_send)(wait)
 
 
-def scratch_of(T, D, NC, S, TP, DP):
-    TB = T // TP
-    G2 = 2 * S
+def scratch_of(T, D, NC, S, TZ, TX, DP):
+    TP = TZ * TX
+    TB, H = T // TP, D // 2
+    G2, slab = 2 * S, max(128, D // TP)
     v = pltpu.VMEM
     return dict(
-        hb=v((2, T, D), bf16),
+        hb=v((2, TZ, TX, TB, D), bf16),
         n2=v((2, 2 * T, D), bf16),
-        go2=v((2, 2 * T, D), bf16),
-        wz=v((2, D, NC), bf16),
-        wx=v((2, D, NC), bf16),
+        go2=v((2, 2, TZ, TX, TB, D), bf16),
+        wz=v((2, NC, D), bf16),
+        wx=v((2, NC, D), bf16),
         wbc=v((2, D, G2), bf16),
         wdt=v((2, 128, D), bf16),
         wout=v((2, NC, D), bf16),
@@ -136,7 +142,6 @@
         cex=v((T, NC), f32),
         ee=v((2, T, NC), f32),
         tl=v((2, T, NC), f32),
-        stp=v((2, 8, T), f32),
         arow=v((2, 8, T), f32),
         sgd=v((2, 8, T), f32),
         yv=v((T, NC), f32),
@@ -147,19 +152,25 @@
         sq=v((T, NC), bf16),
         sq2=v((T, NC), bf16),
         gni=v((T, NC), f32),
-        s0=v((2, S, NC), f32),
-        stS=v((4, S + 16, 256), bf16),
-        stR=v((4, DP - 1, S + 16, 256), bf16),
-        arS=v((2, 8, T), f32),
-        arR=v((2, TP - 1, 8, T), f32),
-        us=v((4, T, D), bf16),
-        ur=v((4, TP - 1, TB, D), bf16),
-        own=v((4, TB, D), bf16),
+        s0=v((2, NC, S), f32),
+        eT=v((2, 8, S), f32),
+        stS=v((4, NC + 16, S), bf16),
+        stR=v((4, DP - 1, NC + 16, S), bf16),
+        arS=v((2, 8, T // 2), f32),
+        arR=v((2, TP - 1, 8, T // 2), f32),
+        us=v((4, TZ, TX, TB, D), bf16),
+        r1a=v((4, TZ - 1, TX, TB, H), bf16),
+        r1b=v((4, TX - 1, TZ, TB, H), bf16),
+        ma=v((4, TX, TB, H), bf16),
+        mb=v((4, TZ, TB, H), bf16),
+        r2a=v((4, TX - 1, TB, H), bf16),
+        r2b=v((4, TZ - 1, TB, H), bf16),
+        own=v((2, TB, D), bf16),
         u0=v((TB, D), f32),
         rex=v((2, T, NC), f32),
         kex=v((T, NC), f32),
-        crossS=v((TB, 256), f32),
-        cross=v((T, 256), f32),
+        crossS=v((TB, 128), f32),
+        cross=v((T, 128), f32),
         gm=v((T, NC), f32),
         eg=v((T, NC), bf16),
         gz2=v((2, 2 * T, NC), bf16),
@@ -181,19 +192,18 @@
         gbr=v((2, TP - 1, TB, G2), bf16),
         gbo=v((2, TB, G2), bf16),
         gb2=v((2, 2 * T, G2), bf16),
-        nT=v((D, 2 * T), bf16),
-        dzS=v((2, D, NC), bf16),
-        dzR=v((2, DP - 1, D // DP, NC), bf16),
-        dzO=v((2, D // DP, NC), bf16),
-        dxS=v((2, D, NC), bf16),
-        dxR=v((2, DP - 1, D // DP, NC), bf16),
-        dxO=v((2, D // DP, NC), bf16),
+        dzS=v((2, NC, D), bf16),
+        dzR=v((2, DP - 1, NC // DP, D), bf16),
+        dzO=v((2, NC // DP, D), bf16),
+        dxS=v((2, NC, D), bf16),
+        dxR=v((2, DP - 1, NC // DP, D), bf16),
+        dxO=v((2, NC // DP, D), bf16),
         doS=v((2, NC, D), bf16),
         doR=v((2, DP - 1, NC // DP, D), bf16),
         doO=v((2, NC // DP, D), bf16),
-        dbS=v((2, D // TP, G2), bf16),
-        dbR=v((2, DP - 1, D // TP, G2), bf16),
-        dbO=v((2, D // TP, G2), bf16),
+        dbS=v((2, slab, G2), bf16),
+        dbR=v((2, DP - 1, slab, G2), bf16),
+        dbO=v((2, slab, G2), bf16),
         dtS=v((2, 8, D), f32),
         dtR=v((2, DP - 1, 8, D), f32),
         gpS=v((2, 8, 384), f32),
@@ -202,8 +212,8 @@
         fpR=v((2, 2 * DP - 1, 24, 384), f32),
         w_sems=pltpu.SemaphoreType.DMA((6, 2)),
         l_sems=pltpu.SemaphoreType.DMA((24,)),
-        send_sems=pltpu.SemaphoreType.DMA((96,)),
-        recv_sems=pltpu.SemaphoreType.DMA((96,)),
+        send_sems=pltpu.SemaphoreType.DMA((160,)),
+        recv_sems=pltpu.SemaphoreType.DMA((160,)),
     )
 
 
@@ -231,12 +241,17 @@
 
 def kernel(geo, names, *refs):
     k = types.SimpleNamespace(**dict(zip(names, refs)))
-    T, D, NC, S, TP, DP = geo
-    TB, G2, INNER = T // TP, 2 * S, NC * TP
+    T, D, NC, S, TZ, TX, DP = geo
+    TP = TZ * TX
+    TB, G2, INNER, H = T // TP, 2 * S, NC * TP, D // 2
+    FIRST, SECOND = slice(0, H), slice(H, D)
+    slab = max(128, D // TP)
+    slabs = D // slab
     c, d, t = lax.axis_index("pipe"), lax.axis_index("dp"), lax.axis_index("tensor")
     other = 1 - c
+    tz, tx = t // TX, lax.rem(t, TX)
     mine = pl.ds(pl.multiple_of(t * TB, TB), TB)
-    ids = iter(range(96))
+    ids = iter(range(160))
     pending = []
 
     def op(sent, received, when_send=None, when_recv=None):
@@ -255,6 +270,17 @@
 
         lax.fori_loop(first, TP, step, 0)
 
+    barrier = pltpu.get_barrier_semaphore()
+
+    def greet(**device):
+        pl.semaphore_signal(barrier, inc=1, device_id=device, device_id_type=MESH)
+
+    peers(lambda j, to: greet(pipe=other, tensor=to), 0)
+    peers(lambda j, to: greet(tensor=to))
+    for j in range(1, DP):
+        greet(dp=lax.rem(d + j, DP))
+        greet(pipe=other, dp=lax.rem(d + j, DP))
+
     in_tokens = local(k.i_tokens.at[c], k.hb.at[0], 0)
     in_tokens.start()
     weights = [("wx", 0), ("wbc", 1), ("wdt", 2), ("wz", 3), ("wout", 4)]
@@ -265,9 +291,9 @@
 
     for name, i in weights:
         pltpu.make_async_copy(getattr(k, "i_" + name).at[0], held(name), k.w_sems.at[i, c]).start()
-    in_cot = local(k.i_cot.at[c], k.go2.at[1, 0:T], 1)
+    in_cot = local(k.i_cot.at[c], k.go2.at[1, 0], 1)
     in_cot.start()
-    in_cot_other = local(k.i_cot.at[other], k.go2.at[1, T : 2 * T], 2)
+    in_cot_other = local(k.i_cot.at[other], k.go2.at[1, 1], 2)
     in_cot_other.start()
 
     pk = k.pkown
@@ -287,42 +313,6 @@
     pk[7:8, 0:NC] = skip
     pltpu.make_async_copy(k.pkown, k.pk.at[c], k.w_sems.at[5, c]).start()
 
-    barrier = pltpu.get_barrier_semaphore()
-
-    def greet(**device):
-        pl.semaphore_signal(barrier, inc=1, device_id=device, device_id_type=MESH)
-
-    peers(lambda j, to: greet(tensor=to))
-    peers(lambda j, to: greet(pipe=other, tensor=to), 0)
-    for j in range(1, DP):
-        greet(dp=lax.rem(d + j, DP))
-        greet(pipe=other, dp=lax.rem(d + j, DP))
-    pl.semaphore_wait(barrier, 2 * TP - 1 + 2 * (DP - 1))
-
-    w_sent = []
-
-    def give(src, dst, i):
-        send = k.send_sems.at[next(ids)]
-        copy = pltpu.make_async_remote_copy(
-            src_ref=src,
-            dst_ref=dst,
-            send_sem=send,
-            recv_sem=k.w_sems.at[i, c],
-            device_id={"pipe": other},
-            device_id_type=MESH,
-        )
-        copy.start()
-        w_sent.append(copy)
-
-    give(k.pkown, k.pk.at[c], 5)
-    for name, i in weights:
-        give(getattr(k, "i_" + name).at[0], held(name), i)
-
-    def have(name, i, l):
-        ref = getattr(k, name)
-        ref = ref.at[l, 0:16] if name == "wdt" else ref.at[l]
-        pltpu.make_async_copy(ref, ref, k.w_sems.at[i, l]).wait()
-
     first_end = k.i_seq[c, 0]
     second_end = first_end + k.i_seq[c, 1]
 
@@ -344,6 +334,32 @@
     for l in range(2):
         k.wdt[l, 16:128, :] = jnp.zeros((112, D), bf16)
 
+    pl.semaphore_wait(barrier, 2 * TP - 1 + 2 * (DP - 1))
+
+    w_sent = []
+
+    def give(src, dst, i):
+        send = k.send_sems.at[next(ids)]
+        copy = pltpu.make_async_remote_copy(
+            src_ref=src,
+            dst_ref=dst,
+            send_sem=send,
+            recv_sem=k.w_sems.at[i, c],
+            device_id={"pipe": other},
+            device_id_type=MESH,
+        )
+        copy.start()
+        w_sent.append(copy)
+
+    give(k.pkown, k.pk.at[c], 5)
+    for name, i in weights:
+        give(getattr(k, "i_" + name).at[0], held(name), i)
+
+    def have(name, i, l):
+        ref = getattr(k, name)
+        ref = ref.at[l, 0:16] if name == "wdt" else ref.at[l]
+        pltpu.make_async_copy(ref, ref, k.w_sems.at[i, l]).wait()
+
     def running(x, backward=False):
         p = jnp.concatenate(parts3(x) + [jnp.zeros_like(x)], axis=0).astype(bf16)
         y = nt(p, k.tri[...]) if backward else nn(p, k.tri[...])
@@ -354,47 +370,112 @@
 
     per_head = ones_where(iota((8, NC), 0) == iota((8, NC), 1) // HD)
 
-    def joined(slot, have_k):
-        total, through = jnp.zeros((S, NC), f32), jnp.ones((1, NC), f32)
+    def states_to(slot, backward):
+        ops = []
         for j in range(1, DP):
-            part = k.stR[slot, j - 1, 0:S, 0:NC].astype(f32)
-            decay = k.stR[slot, j - 1, S : S + 16, 0:NC].astype(f32)[0:1]
-            total = total + (through * have_k(j)) * part
-            through = through * decay
-        return total
+            src, dst = k.stS.at[slot], k.stR.at[slot, j - 1]
+            up, down = d + j < DP, d >= j
+            made = op(src, dst, down if backward else up, up if backward else down)
+            to = lax.rem(d + (DP - j if backward else j), DP)
+            pl.when(down if backward else up)(lambda: made.to(src, dst, dp=to))
+            ops.append(made)
+        return ops
+
+    def joined(slot, backward):
+        blocks = [jnp.zeros((HD, S), f32)] * 3
+        through = jnp.ones((8, S), f32)
+        for j in range(1, DP):
+            there = d + j < DP if backward else d >= j
+            part = k.stR[slot, j - 1, 0:NC, :].astype(f32)
+            for h in range(3):
+                term = through[h : h + 1] * part[HD * h : HD * h + HD]
+                blocks[h] = blocks[h] + jnp.where(there, term, 0.0)
+            decay = k.stR[slot, j - 1, NC : NC + 16, :].astype(f32)[0:8]
+            through = through * jnp.where(there, decay, 0.0)
+        return jnp.concatenate(blocks, axis=0)
+
+    def z_peers(body):
+        for j in sorted(range(1, TZ), key=lambda j: min(j, TZ - j)):
+            q = lax.rem(tz + j, TZ)
+            body(j, q, q * TX + tx)
+
+    def x_peers(body):
+        for j in sorted(range(1, TX), key=lambda j: min(j, TX - j)):
+            p = lax.rem(tx + j, TX)
+            body(j, p, tz * TX + p)
 
     def scatter(slot):
-        made = op(k.ur.at[slot], k.ur.at[slot])
-
-        def body(j, to):
-            rows = pl.ds(pl.multiple_of(to * TB, TB), TB)
-            made.to(k.us.at[slot, rows], k.ur.at[slot, j - 1], tensor=to)
-
-        peers(body)
-        return made
+        a1, b1 = (op(r.at[slot], r.at[slot]) for r in (k.r1a, k.r1b))
+        z_peers(lambda j, q, to: a1.to(k.us.at[slot, q, :, :, FIRST], k.r1a.at[slot, j - 1], tensor=to))
+        x_peers(lambda j, p, to: b1.to(k.us.at[slot, :, p, :, SECOND], k.r1b.at[slot, j - 1], tensor=to))
+        return a1, b1
+
+    def scatter_on(slot, made):
+        a2, b2 = (op(r.at[slot], r.at[slot]) for r in (k.r2a, k.r2b))
+        made[0].arrived()
+        total = k.us[slot, tz, :, :, FIRST].astype(f32)
+        for j in range(TZ - 1):
+            total = total + k.r1a[slot, j].astype(f32)
+        k.ma[slot] = total.astype(bf16)
+        x_peers(lambda j, p, to: a2.to(k.ma.at[slot, p], k.r2a.at[slot, j - 1], tensor=to))
+        made[1].arrived()
+        total = k.us[slot, :, tx, :, SECOND].astype(f32)
+        for j in range(TX - 1):
+            total = total + k.r1b[slot, j].astype(f32)
+        k.mb[slot] = total.astype(bf16)
+        z_peers(lambda j, q, to: b2.to(k.mb.at[slot, q], k.r2b.at[slot, j - 1], tensor=to))
+        return a2, b2
 
     def summed(made, slot):
-        made.arrived()
-        total = k.us[slot, mine, :].astype(f32)
-        for j in range(TP - 1):
-            total = total + k.ur[slot, j].astype(f32)
-        return total
+        made[0].arrived()
+        first = k.ma[slot, tx].astype(f32)
+        for j in range(TX - 1):
+            first = first + k.r2a[slot, j].astype(f32)
+        made[1].arrived()
+        second = k.mb[slot, tz].astype(f32)
+        for j in range(TZ - 1):
+            second = second + k.r2b[slot, j].astype(f32)
+        return jnp.concatenate([first, second], axis=1)
+
+    def gather(buffer, rows):
+        buffer[tz, tx] = rows
+        done = buffer.at[0, 0 : TX - 1, :, FIRST], buffer.at[0 : TZ - 1, 0, :, SECOND]
+        a1, b1 = (op(r, r) for r in done)
+        first, second = buffer.at[tz, tx, :, FIRST], buffer.at[tz, tx, :, SECOND]
+        x_peers(lambda j, p, to: a1.to(first, first, tensor=to))
+        z_peers(lambda j, q, to: b1.to(second, second, tensor=to))
+        return a1, b1
+
+    def gather_on(buffer, made):
+        done = buffer.at[0 : TZ - 1, :, :, FIRST], buffer.at[:, 0 : TX - 1, :, SECOND]
+        a2, b2 = (op(r, r) for r in done)
+        first, second = buffer.at[tz, :, :, FIRST], buffer.at[:, tx, :, SECOND]
+        made[0].arrived()
+        z_peers(lambda j, q, to: a2.to(first, first, tensor=to))
+        made[1].arrived()
+        x_peers(lambda j, p, to: b2.to(second, second, tensor=to))
+        return a2, b2
+
+    def both(made):
+        for m in made:
+            m.arrived()
 
     def forward(l):
         have("pk", 5, l)
 
         def norm(r, i):
-            h = k.hb[l, r, :].astype(f32)
+            pair = pl.ds(lax.rem(i, TX // 2) * 2, 2)
+            h = k.hb[l, i // (TX // 2), pair].reshape(2 * TB, D).astype(f32)
             scale = lax.rsqrt(jnp.mean(h * h, axis=1, keepdims=True) + EPS)
             k.n2[l, r, :] = (h * scale * k.pk[l, 0:1, :]).astype(bf16)
 
-        over(T, 32, norm)
+        over(T, 2 * TB, norm)
         send_n = op(k.n2.at[l, 0:T], k.n2.at[l, T : 2 * T], c != l, c == l)
         pl.when(c != l)(
             lambda: send_n.to(k.n2.at[l, 0:T], k.n2.at[l, T : 2 * T], pipe=other)
         )
         have("wx", 0, l)
-        k.xe[l, 8 : 8 + T, :] = nn(k.n2[l, 0:T, :], k.wx[l])
+        k.xe[l, 8 : 8 + T, :] = nt(k.n2[l, 0:T, :], k.wx[l])
         have("wbc", 1, l)
         k.be[l, 8 : 8 + T, :] = nn(k.n2[l, 0:T, :], k.wbc[l])
         halo_x = op(k.xe.at[l, T : T + 8], k.xe.at[l, 0:8])
@@ -407,9 +488,8 @@
         step = jnp.maximum(dtp, 0.0) + jnp.log1p(jnp.exp(-jnp.abs(dtp)))
         a = -jnp.exp(k.pk[l, 8:16, T : 2 * T]) * step
         run = running(a)
-        k.stp[l], k.arow[l], k.sgd[l] = step, a, sigmoid(dtp)
-        have("wz", 3, l)
-        k.gate[l] = nn(k.n2[l, 0:T, :], k.wz[l])
+        k.arow[l], k.sgd[l] = a, sigmoid(dtp)
+        k.eT[l] = jnp.broadcast_to(jnp.exp(run[:, T - 1 : T]) * k.pmask[T - 1 : T, 0:1], (8, S))
         cols = columns_of([run, step])
         k.cex[...] = nn(cols, pick(0, NC, heads_of))
         k.dte[l] = nn(cols, pick(1, NC, heads_of))
@@ -449,11 +529,12 @@
                     k.Cm[l, r, :] = act[:, S:G2].astype(bf16)
 
         over(T, RB, conv)
-        k.stS[l, 0:S, 0:NC] = tn(k.Bm[l], k.xtail[l]).astype(bf16)
-        k.stS[l, S : S + 16, 0:NC] = jnp.broadcast_to(k.ee[l, T - 1 : T, :], (16, NC)).astype(bf16)
-        states = op(k.stR.at[l], k.stR.at[l])
-        for j in range(1, DP):
-            states.to(k.stS.at[l], k.stR.at[l, j - 1], dp=lax.rem(d + j, DP))
+        k.stS[l, 0:NC, :] = tn(k.xtail[l], k.Bm[l]).astype(bf16)
+        ends = jnp.concatenate([k.eT[l], jnp.zeros((8, S), f32)], axis=0)
+        k.stS[l, NC : NC + 16, :] = ends.astype(bf16)
+        states = states_to(l, False)
+        have("wz", 3, l)
+        k.gate[l] = nt(k.n2[l, 0:T, :], k.wz[l])
         k.G[l] = nt(k.Cm[l], k.Bm[l])
 
         def mixing(r, i):
@@ -467,10 +548,10 @@
         k.yv[...] = nn(k.Wc[l], k.blk[...])
         if l == 1:
             have("wout", 4, l)
-            k.gni[...] = nt(k.go2[1, 0:T, :], k.wout[1])
-        states.arrived()
-        k.s0[l] = joined(l, lambda j: jnp.where(d >= j, 1.0, 0.0))
-        k.yin[l] = nn(k.Cm[l], k.s0[l].astype(bf16)) * k.ee[l]
+            k.gni[...] = nt(k.go2[1, 0].reshape(T, D), k.wout[1])
+        both(states)
+        k.s0[l] = joined(l, False)
+        k.yin[l] = nt(k.Cm[l], k.s0[l].astype(bf16)) * k.ee[l]
 
         def gating(r, i):
             z = k.gate[l, r, :]
@@ -489,21 +570,24 @@
         sums = nt(ones_where(row == 0), k.sq[...])
         if l == 1:
             sums = sums + nt(ones_where(row == 1), k.sq2[...])
-        k.arS[l] = sums
+        halves = [sums[0:1, 0 : T // 2], sums[0:1, T // 2 :], sums[1:2, 0 : T // 2], sums[1:2, T // 2 :]]
+        k.arS[l] = jnp.concatenate(halves + [jnp.zeros((4, T // 2), f32)], axis=0)
         small = op(k.arR.at[l], k.arR.at[l])
         peers(lambda j, to: small.to(k.arS.at[l], k.arR.at[l, j - 1], tensor=to))
         if l == 0:
             have("wout", 4, l)
         for j in range(D // 256):
             lanes = slice(256 * j, 256 * j + 256)
-            k.us[l, :, lanes] = nn(k.gg[l], k.wout[l, :, lanes]).astype(bf16)
+            part = nn(k.gg[l], k.wout[l, :, lanes]).astype(bf16)
+            k.us[l, :, :, :, lanes] = part.reshape(TZ, TX, TB, 256)
         made = scatter(l)
         small.arrived()
         total = k.arS[l]
         for j in range(TP - 1):
             total = total + k.arR[l, j]
-        r = lax.rsqrt(total[0:1] / INNER + EPS)
-        factor = r * r * r * (total[1:2] / INNER)
+        squares = jnp.concatenate([total[0:1], total[1:2]], axis=1)
+        r = lax.rsqrt(squares / INNER + EPS)
+        factor = r * r * r * (jnp.concatenate([total[2:3], total[3:4]], axis=1) / INNER)
         cols = columns_of([jnp.concatenate([r, factor, jnp.zeros((6, T), f32)], axis=0)])
         k.rex[l] = nn(cols, pick(0, NC, lambda lane: 0 * lane))
         if l == 1:
@@ -514,32 +598,52 @@
         total = summed(made, l)
         if l == 0:
             k.u0[...] = total
-        out = k.hb[l, mine, :].astype(f32) + k.rex[l, mine, 0:1] * total
-        k.own[l] = out.astype(bf16)
-
-    def spread_out(slot, out, l):
-        near = op(out.at[0, 0, 0 : T - TB], out.at[0, 0, 0 : T - TB], c == l, c == l)
-        far = op(out.at[0, 0, 0:T], out.at[0, 0, 0:T], c != l, c == l)
-        dst = out.at[0, c, mine]
-        keep = local(k.own.at[slot], dst, 8 + slot)
+        return (k.hb[l, tz, tx].astype(f32) + k.rex[l, mine, 0:1] * total).astype(bf16)
+
+    def spread(src, out, l, i):
+        near_a, near_b = out.at[0, 0, 0, 0 : TX - 1, :, FIRST], out.at[0, 0, 0 : TZ - 1, 0, :, SECOND]
+        far_a, far_b = out.at[0, 0, 0, 0:TX, :, FIRST], out.at[0, 0, 0:TZ, 0, :, SECOND]
+        na, nb = (op(x, x, c == l, c == l) for x in (near_a, near_b))
+        fa, fb = (op(x, x, c != l, c == l) for x in (far_a, far_b))
+        dst = out.at[0, c, tz, tx]
+        first, second = dst.at[:, FIRST], dst.at[:, SECOND]
+        keep = local(src, dst, i)
 
         @pl.when(c == l)
         def _():
-            peers(lambda j, to: near.to(k.own.at[slot], dst, tensor=to))
+            x_peers(lambda j, p, to: na.to(src.at[:, FIRST], first, tensor=to))
+            z_peers(lambda j, q, to: nb.to(src.at[:, SECOND], second, tensor=to))
             keep.start()
 
         @pl.when(c != l)
         def _():
-            peers(lambda j, to: far.to(k.own.at[slot], dst, pipe=other, tensor=to), 0)
-
-        return near, far, lambda: pl.when(c == l)(keep.wait)
-
-    def gather_in(slot, buffer):
-        made = op(buffer.at[0 : T - TB], buffer.at[0 : T - TB])
-        dst = buffer.at[mine]
-        peers(lambda j, to: made.to(k.own.at[slot], dst, tensor=to))
-        dst[...] = k.own[slot]
-        return made
+            for p in range(TX):
+                fa.to(src.at[:, FIRST], first, pipe=other, tensor=tz * TX + p)
+            for q in range(TZ):
+                fb.to(src.at[:, SECOND], second, pipe=other, tensor=q * TX + tx)
+
+        return na, nb, fa, fb, keep
+
+    def spread_on(out, l, made):
+        na, nb, fa, fb, keep = made
+        done_a, done_b = out.at[0, 0, 0 : TZ - 1, :, :, FIRST], out.at[0, 0, :, 0 : TX - 1, :, SECOND]
+        ops = [op(x, x, c == l, c == l) for x in (done_a, done_b, done_a, done_b)]
+        mine_a, mine_b = out.at[0, c, tz, :, :, FIRST], out.at[0, c, :, tx, :, SECOND]
+        that_a, that_b = out.at[0, other, tz, :, :, FIRST], out.at[0, other, :, tx, :, SECOND]
+
+        @pl.when(c == l)
+        def _():
+            keep.wait()
+            na.take()
+            z_peers(lambda j, q, to: ops[0].to(mine_a, mine_a, tensor=to))
+            nb.take()
+            x_peers(lambda j, p, to: ops[1].to(mine_b, mine_b, tensor=to))
+            fa.take()
+            z_peers(lambda j, q, to: ops[2].to(that_a, that_a, tensor=to))
+            fb.take()
+            x_peers(lambda j, p, to: ops[3].to(that_b, that_b, tensor=to))
+
+        return ops
 
     def hand_out(src, out, l, i):
         far = op(src, out.at[0, 0], c != l, c == l)
@@ -555,9 +659,9 @@
 
         return far, lambda: pl.when(c == l)(keep.wait)
 
-    def backward(l):
+    def backward(l, meanwhile):
         if l == 0:
-            k.gni[...] = nt(k.go2[0, 0:T, :], k.wout[0])
+            k.gni[...] = nt(k.go2[0, 0].reshape(T, D), k.wout[0])
 
         def gates(r, i, sums):
             z = k.gate[l, r, :]
@@ -566,7 +670,7 @@
             if l == 1:
                 factor = k.kex[r, :]
             else:
-                factor = rx * rx * rx * (k.cross[r, 0:NC] / INNER)
+                factor = rx * rx * rx * (k.cross[r, 0:1] / INNER)
             gain = k.pk[l, 6:7, 0:NC]
             g = rx * (gn * gain) - gated * factor
             gm = g * z * s
@@ -592,11 +696,9 @@
         k.fpS[l] = jnp.zeros((24, 384), f32)
         k.fpS[l, 13:14, 0:NC] = by_gain
         k.fpS[l, 14:15, 0:NC] = by_skip
-        k.stS[2 + l, 0:S, 0:NC] = tn(k.Cm[l], k.eg[...]).astype(bf16)
-        k.stS[2 + l, S : S + 16, 0:NC] = k.stS[l, S : S + 16, 0:NC]
-        states = op(k.stR.at[2 + l], k.stR.at[2 + l])
-        for j in range(1, DP):
-            states.to(k.stS.at[2 + l], k.stR.at[2 + l, j - 1], dp=lax.rem(d + DP - j, DP))
+        k.stS[2 + l, 0:NC, :] = tn(k.eg[...], k.Cm[l]).astype(bf16)
+        k.stS[2 + l, NC : NC + 16, :] = k.stS[l, NC : NC + 16, :]
+        states = states_to(2 + l, True)
         dxt = jnp.zeros((T, NC), f32)
         for h in range(3):
             part = k.blk[h * T : h * T + T, :]
@@ -617,14 +719,17 @@
         for h in range(3):
             one = ones_where(iota((8, T), 0) == h)
             flow = flow + nt(one, k.Pb[h]) - nn(one, k.Pb[h])
-        states.arrived()
-        after = joined(2 + l, lambda j: jnp.where(d + j < DP, 1.0, 0.0))
-        through = jnp.sum(after * k.s0[l], axis=0, keepdims=True) * k.ee[l, T - 1 : T, :]
-        constant = jnp.sum(per_head.astype(f32) * through, axis=1, keepdims=True)
+        meanwhile()
+        both(states)
+        after = joined(2 + l, True)
+        through = after * k.s0[l]
+        rows = [jnp.sum(through[HD * h : HD * h + HD], axis=0, keepdims=True) for h in range(3)]
+        rows = jnp.concatenate(rows + [jnp.zeros((5, S), f32)], axis=0)
+        constant = jnp.sum(rows * k.eT[l], axis=1, keepdims=True)
         after = after.astype(bf16)
-        k.bes[...] = nn(k.Bm[l], after)
-        k.dbc[:, 0:S] = tn(k.dG[...], k.Cm[l]) + nt(k.xtail[l], after)
-        k.dbc[:, S:G2] = nn(k.dG[...], k.Bm[l]) + nt(k.eg[...], k.s0[l].astype(bf16))
+        k.bes[...] = nt(k.Bm[l], after)
+        k.dbc[:, 0:S] = tn(k.dG[...], k.Cm[l]) + nn(k.xtail[l], after)
+        k.dbc[:, S:G2] = nn(k.dG[...], k.Bm[l]) + nn(k.eg[...], k.s0[l].astype(bf16))
 
         def inputs(r, i):
             x, gm, dte = k.X[l, r, :], k.gm[r, :], k.dte[l, r, :]
@@ -703,26 +808,26 @@
         gdt_cols = jnp.concatenate([gdt, jnp.zeros((120, T), f32)], axis=0).T.astype(bf16)
         for j in range(D // 256):
             at = slice(256 * j, 256 * j + 256)
-            part = nt(k.gz2[l, 0:T, :], k.wz[l, at, :]) + nt(k.gx2[l, 0:T, :], k.wx[l, at, :])
+            part = nn(k.gz2[l, 0:T, :], k.wz[l, :, at]) + nn(k.gx2[l, 0:T, :], k.wx[l, :, at])
             part = part + nt(k.gbp[l], k.wbc[l, at, :]) + nn(gdt_cols, k.wdt[l, :, at])
-            k.us[2 + l, :, at] = part.astype(bf16)
+            k.us[2 + l, :, :, :, at] = part.astype(bf16).reshape(TZ, TX, TB, 256)
         return scatter(2 + l), bc
 
     def input_rows(l, made):
         gn = summed(made, 2 + l)
-        h = k.hb[l, mine, :].astype(f32)
+        h = k.hb[l, tz, tx].astype(f32)
         scale = lax.rsqrt(jnp.mean(h * h, axis=1, keepdims=True) + EPS)
         weighted = gn * k.pk[l, 0:1, :]
         inner = jnp.sum(weighted * h, axis=1, keepdims=True)
         gh = scale * weighted - h * (scale * scale * scale * (1.0 / D) * inner)
-        low = (k.go2[l, mine, :].astype(f32) + gh).astype(bf16)
-        k.own[2 + l] = low
+        low = (k.go2[l, 0, tz, tx].astype(f32) + gh).astype(bf16)
         by_pre = jnp.sum(gn * h * scale, axis=0, keepdims=True)
         for j in range(4):
             k.gpS[l, j : j + 1, :] = by_pre[:, 384 * j : 384 * j + 384]
         if l == 1:
             sums = jnp.sum(low.astype(f32) * k.u0[...], axis=1, keepdims=True)
-            k.crossS[...] = jnp.broadcast_to(sums, (TB, 256))
+            k.crossS[...] = jnp.broadcast_to(sums, (TB, 128))
+        return low
 
     def operands(l):
         pairs = [(k.gz2.at[l, 0:T], k.gz2.at[l, T : 2 * T])]
@@ -791,55 +896,56 @@
 
         return spread, finish, (own.at[l], out.at[0, rows])
 
-    def weight_grads(l, n_op, factor_ops, bc_ops, go_op):
-        dz, start_z = ring(l, "dz", D // DP)
-        dx, start_x = ring(l, "dx", D // DP)
+    def weight_grads(l, n_op, factor_ops, go_op):
+        dz, start_z = ring(l, "dz", NC // DP)
+        dx, start_x = ring(l, "dx", NC // DP)
         do, start_o = ring(l, "do", NC // DP)
         dt_made = op(k.dtR.at[l], k.dtR.at[l], c == l, c == l)
-        db_made = op(k.dbR.at[l], k.dbR.at[l], c == l, c == l)
 
         @pl.when(c == l)
         def _():
-            pltpu.make_async_copy(n_op.received, n_op.received, n_op.recv).wait()
+            n_op.take()
             for made in factor_ops:
-                pltpu.make_async_copy(made.received, made.received, made.recv).wait()
+                made.take()
             if go_op is not None:
-                pltpu.make_async_copy(go_op.received, go_op.received, go_op.recv).wait()
-            for j in range(D // 128):
-                at = slice(128 * j, 128 * j + 128)
-                k.nT[at, :] = k.n2[l, :, at].T
-            k.dxS[l] = nn(k.nT[...], k.gx2[l]).astype(bf16)
-            start_x()
-            k.dzS[l] = nn(k.nT[...], k.gz2[l]).astype(bf16)
-            start_z()
-            for j in range(D // 256):
-                at = slice(256 * j, 256 * j + 256)
-                k.doS[l, :, at] = tn(k.ni2[l], k.go2[l, :, at]).astype(bf16)
-            start_o()
+                go_op.take()
+            for start, dst, left, right in (
+                (start_x, k.dxS, k.gx2, k.n2),
+                (start_z, k.dzS, k.gz2, k.n2),
+                (start_o, k.doS, k.ni2, k.go2),
+            ):
+                for j in range(D // 256):
+                    at = slice(256 * j, 256 * j + 256)
+                    dst[l, :, at] = tn(left[l], right[l, ..., at].reshape(2 * T, 256)).astype(bf16)
+                start()
             steps = jnp.concatenate([k.gdt2[l], jnp.zeros((8, 2 * T), f32)], axis=0).astype(bf16)
             k.dtS[l] = nn(steps, k.n2[l])[0:8]
             for j in range(1, DP):
                 dt_made.to(k.dtS.at[l], k.dtR.at[l, j - 1], dp=lax.rem(d + j, DP))
+
+        return dz, dx, do, dt_made
+
+    def bc_grads(l, bc_ops):
+        db_made = op(k.dbR.at[l], k.dbR.at[l], c == l, c == l)
+
+        @pl.when(c == l)
+        def _():
             for made in bc_ops:
-                pltpu.make_async_copy(made.received, made.received, made.recv).wait()
-            part = pl.ds(pl.multiple_of(t * (D // TP), D // TP), D // TP)
-            k.dbS[l] = nn(k.nT[part, :], k.gb2[l]).astype(bf16)
+                made.take()
+            part = pl.ds(pl.multiple_of(lax.rem(t, slabs) * slab, slab), slab)
+            k.dbS[l] = tn(k.n2[l, :, part], k.gb2[l]).astype(bf16)
             for j in range(1, DP):
                 db_made.to(k.dbS.at[l], k.dbR.at[l, j - 1], dp=lax.rem(d + j, DP))
 
-        return dz, dx, do, dt_made, db_made
+        return db_made
 
     def weight_ends(l, made):
-        dz, dx, do, dt_made, db_made = made
+        dz, dx, do, dt_made = made
         ends = [
-            ring_end(l, "dx", dx, k.o_wx, D // DP),
-            ring_end(l, "dz", dz, k.o_wz, D // DP),
+            ring_end(l, "dx", dx, k.o_wx, NC // DP),
+            ring_end(l, "dz", dz, k.o_wz, NC // DP),
             ring_end(l, "do", do, k.o_wout, NC // DP),
         ]
-        slab = D // TP
-        rows = pl.ds(pl.multiple_of(t * slab, slab), slab)
-        count = slab * (TP - 1)
-        spread = op(k.o_wbc.at[0, 0:count], k.o_wbc.at[0, 0:count], c == l, c == l)
 
         @pl.when(c == l)
         def _():
@@ -848,14 +954,6 @@
                 finish()
                 copies.append(local(src, dst, 12 + i))
                 copies[-1].start()
-            db_made.arrived()
-            total = k.dbS[l].astype(f32)
-            for j in range(DP - 1):
-                total = total + k.dbR[l, j].astype(f32)
-            k.dbO[l] = total.astype(bf16)
-            peers(lambda j, to: spread.to(k.dbO.at[l], k.o_wbc.at[0, rows], tensor=to))
-            copies.append(local(k.dbO.at[l], k.o_wbc.at[0, rows], 15))
-            copies[-1].start()
             dt_made.arrived()
             total = k.dtS[l]
             for j in range(DP - 1):
@@ -864,7 +962,32 @@
             for copy in copies:
                 copy.wait()
 
-        return [e[0] for e in ends] + [spread]
+        return [e[0] for e in ends]
+
+    def bc_ends(l, db_made):
+        rows = pl.ds(pl.multiple_of(lax.rem(t, slabs) * slab, slab), slab)
+        owner, reader = (c == l) & (t < slabs), (c == l) & (t >= slabs)
+        sent = k.n2.at[l, 0 : slab * (TP - 1) * G2 // D]
+        from_rest = k.o_wbc.at[0, 0 : D - slab]
+        spread = op(sent, from_rest, owner, owner)
+        spread_all = spread.beside(k.o_wbc.at[0], reader)
+
+        @pl.when(c == l)
+        def _():
+            db_made.arrived()
+            total = k.dbS[l].astype(f32)
+            for j in range(DP - 1):
+                total = total + k.dbR[l, j].astype(f32)
+            k.dbO[l] = total.astype(bf16)
+            keep = local(k.dbO.at[l], k.o_wbc.at[0, rows], 15)
+
+            @pl.when(t < slabs)
+            def _():
+                peers(lambda j, to: spread.to(k.dbO.at[l], k.o_wbc.at[0, rows], tensor=to))
+                keep.start()
+                keep.wait()
+
+        return [spread, spread_all]
 
     def small_start(l):
         made = op(k.gpR.at[l], k.gpR.at[l])
@@ -905,77 +1028,126 @@
 
     in_tokens.wait()
     made, n_op0 = forward(0)
-    section_rows(0, made)
-    gather = gather_in(0, k.hb.at[1])
-    gather.arrived()
+    made = scatter_on(0, made)
+    rows = section_rows(0, made)
+    made = gather_on(k.hb.at[1], gather(k.hb.at[1], rows))
+    both(made)
     sec0, sec0_keep = hand_out(k.hb.at[1], k.o_sec, 0, 3)
     in_cot.wait()
     in_cot_other.wait()
     made1, n_op1 = forward(1)
-    made2, bc1 = backward(1)
+    held_back = []
+    made2, bc1 = backward(1, lambda: held_back.append(scatter_on(1, made1)))
     factors1 = operands(1)
-    section_rows(1, made1)
-    sec1 = spread_out(1, k.o_sec, 1)
-    input_rows(1, made2)
-    gather = gather_in(3, k.go2.at[0, 0:T])
+    k.own[1] = section_rows(1, held_back[0])
+    grads1 = weight_grads(1, n_op1, factors1, None)
+    made2 = scatter_on(3, made2)
+    bc_ops1 = bc_total(1, bc1)
+    rows = input_rows(1, made2)
+    made2 = gather(k.go2.at[0, 0], rows)
     cross = op(k.cross.at[0 : T - TB], k.cross.at[0 : T - TB])
     peers(lambda j, to: cross.to(k.crossS, k.cross.at[mine], tensor=to))
     k.cross[mine, :] = k.crossS[...]
+    made2 = gather_on(k.go2.at[0, 0], made2)
     small1 = small_start(1)
-    bc_ops1 = bc_total(1, bc1)
-    gather.arrived()
+    db1 = bc_grads(1, bc_ops1)
+    both(made2)
     cross.arrived()
-    ing1, ing1_keep = hand_out(k.go2.at[0, 0:T], k.o_ing, 1, 4)
-    go_op = op(k.go2.at[0, 0:T], k.go2.at[0, T : 2 * T], c != 0, c == 0)
-    pl.when(c != 0)(
-        lambda: go_op.to(k.go2.at[0, 0:T], k.go2.at[0, T : 2 * T], pipe=other)
-    )
-    grads1 = weight_grads(1, n_op1, factors1, bc_ops1, None)
-    made3, bc0 = backward(0)
+    ing1, ing1_keep = hand_out(k.go2.at[0, 0], k.o_ing, 1, 4)
+    go_op = op(k.go2.at[0, 0], k.go2.at[0, 1], c != 0, c == 0)
+    pl.when(c != 0)(lambda: go_op.to(k.go2.at[0, 0], k.go2.at[0, 1], pipe=other))
+    sec1 = spread(k.own.at[1], k.o_sec, 1, 9)
+    made3, bc0 = backward(0, lambda: held_back.append(spread_on(k.o_sec, 1, sec1)))
     factors0 = operands(0)
+    grads0 = weight_grads(0, n_op0, factors0, go_op)
+    made3 = scatter_on(2, made3)
     bc_ops0 = bc_total(0, bc0)
-    grads0 = weight_grads(0, n_op0, factors0, bc_ops0, go_op)
     packs1 = small_middle(1, small1)
     spreads = weight_ends(1, grads1)
-    input_rows(0, made3)
-    ing0 = spread_out(2, k.o_ing, 0)
+    k.own[0] = input_rows(0, made3)
+    ing0 = spread(k.own.at[0], k.o_ing, 0, 8)
     small0 = small_start(0)
+    db0 = bc_grads(0, bc_ops0)
     spreads += weight_ends(0, grads0)
+    ing0 = spread_on(k.o_ing, 0, ing0)
+    spreads += bc_ends(1, db1)
     packs0 = small_middle(0, small0)
+    spreads += bc_ends(0, db0)
     small_end(1, packs1)
     small_end(0, packs0)
     sec0.arrived()
     sec0_keep()
     ing1.arrived()
     ing1_keep()
-    for near, far, keep in (sec1, ing0):
-        near.arrived()
-        far.arrived()
-        keep()
-    for spread in spreads:
-        spread.arrived()
+    both(held_back[1])
+    both(ing0)
+    both(spreads)
     for copy in w_sent:
         copy.wait_send()
     for made in pending:
         made.left()
 
 
+def finish(geo, sec, ing, dz, dx, dbc, do, dt, pack, *outs):
+    T, D, NC, S = geo
+    G2 = 2 * S
+    o_sec, o_ing, o_pre, o_z, o_x, o_bc, o_dt, o_cx, o_cbc, o_bx, o_bbc, o_dtb = outs[:12]
+    o_alog, o_dsk, o_gain, o_out, sems = outs[12:]
+    copies = [
+        pltpu.make_async_copy(sec, o_sec, sems.at[0]),
+        pltpu.make_async_copy(ing, o_ing, sems.at[1]),
+    ]
+    for copy in copies:
+        copy.start()
+    for src, dst, rows in ((dz, o_z, NC), (dx, o_x, NC), (do, o_out, NC), (dbc, o_bc, D)):
+
+        def widen(r, i, src=src, dst=dst):
+            dst[0, r, :] = src[0, r, :].astype(f32)
+
+        over(rows, 32, widen)
+    for j in range(4):
+        o_pre[:, 384 * j : 384 * j + 384] = pack[j : j + 1, :]
+    for h in range(o_dt.shape[0]):
+        o_dt[h] = dt[h : h + 1, :]
+    o_cx[0] = pack[8:12, 0:NC]
+    o_cbc[0] = pack[4:8, 0:G2]
+    o_bx[...] = pack[12:13, 0:NC]
+    o_bbc[:, 0:128] = pack[4:5, 256:384]
+    o_bbc[:, 128:256] = pack[5:6, 256:384]
+    o_gain[...] = pack[13:14, 0:NC]
+    lane = iota((1, 3), 1)
+    chan = iota((1, NC), 1)
+    b, a, s = (jnp.zeros((1, 3), f32),) * 3
+    for h in range(3):
+        one = lane == h
+        b = jnp.where(one, pack[16 + h : 17 + h, 0:1], b)
+        a = jnp.where(one, pack[16 + h : 17 + h, 128:129], a)
+        by_skip = jnp.where(chan // HD == h, pack[14:15, 0:NC], 0.0)
+        s = jnp.where(one, jnp.sum(by_skip, axis=1, keepdims=True), s)
+    o_dtb[...], o_alog[...], o_dsk[...] = b, a, s
+    for copy in copies:
+        copy.wait()
+
+
 def on_device(sizes, *args):
     (tokens, seq, cot, pre, wz, wx, wbc, wdt, cx, cbc, bx, bbc, dtb, alog, dsk, gain, wout) = args
-    TP, DP = sizes
+    (TZ, TX), DP = sizes
     _, T, D = tokens.shape
+    TB = T // (TZ * TX)
     NC, S = wx.shape[2], wbc.shape[2] // 2
     wdt = jnp.pad(jnp.swapaxes(wdt, 1, 2), ((0, 0), (0, 13), (0, 0)))
-    scratch = scratch_of(T, D, NC, S, TP, DP)
+    wz, wx = jnp.swapaxes(wz, 1, 2), jnp.swapaxes(wx, 1, 2)
+    tokens, cot = (x.reshape(2, TZ, TX, TB, D) for x in (tokens, cot))
+    scratch = scratch_of(T, D, NC, S, TZ, TX, DP)
     names = tuple(INPUTS) + tuple(OUTPUTS) + tuple(scratch)
     any_, vmem, smem = (pl.BlockSpec(memory_space=m) for m in (pl.ANY, pltpu.VMEM, pltpu.SMEM))
     made = pl.pallas_call(
-        functools.partial(kernel, (T, D, NC, S, TP, DP), names),
+        functools.partial(kernel, (T, D, NC, S, TZ, TX, DP), names),
         out_shape=(
-            jax.ShapeDtypeStruct((1, 2, T, D), bf16),
-            jax.ShapeDtypeStruct((1, 2, T, D), bf16),
-            jax.ShapeDtypeStruct((1, D, NC), bf16),
-            jax.ShapeDtypeStruct((1, D, NC), bf16),
+            jax.ShapeDtypeStruct((1, 2, TZ, TX, TB, D), bf16),
+            jax.ShapeDtypeStruct((1, 2, TZ, TX, TB, D), bf16),
+            jax.ShapeDtypeStruct((1, NC, D), bf16),
+            jax.ShapeDtypeStruct((1, NC, D), bf16),
             jax.ShapeDtypeStruct((1, D, 2 * S), bf16),
             jax.ShapeDtypeStruct((1, NC, D), bf16),
             jax.ShapeDtypeStruct((8, D), f32),
@@ -988,30 +1160,40 @@
             collective_id=0, has_side_effects=True, vmem_limit_bytes=60 * 1024 * 1024
         ),
     )(tokens, cot, wz, wx, wbc, wdt, wout, pre, cx, cbc, bx, bbc, gain, seq, dtb, alog, dsk)
-    sec, ing, dwz, dwx, dwbc, dwout, ddt, pack = made
     heads = NC // HD
-    by_skip = pack[14, 0:NC].reshape(1, heads, HD).sum(axis=2)
-    return (
-        sec,
-        ing,
-        pack[0:4].reshape(1, D),
-        dwz.astype(f32),
-        dwx.astype(f32),
-        dwbc.astype(f32),
-        ddt[0:heads].T[None],
-        pack[8:12, 0:NC][None],
-        pack[4:8, 0 : 2 * S][None],
-        pack[12:13, 0:NC],
-        pack[4:6, 256:384].reshape(1, 2 * S),
-        pack[16 : 16 + heads, 0][None],
-        pack[16 : 16 + heads, 128][None],
-        by_skip,
-        pack[13:14, 0:NC],
-        dwout.astype(f32),
-    )
+    done = pl.pallas_call(
+        functools.partial(finish, (T, D, NC, S)),
+        out_shape=(
+            jax.ShapeDtypeStruct((1, 2, TZ, TX, TB, D), bf16),
+            jax.ShapeDtypeStruct((1, 2, TZ, TX, TB, D), bf16),
+            jax.ShapeDtypeStruct((1, D), f32),
+            jax.ShapeDtypeStruct((1, NC, D), f32),
+            jax.ShapeDtypeStruct((1, NC, D), f32),
+            jax.ShapeDtypeStruct((1, D, 2 * S), f32),
+            jax.ShapeDtypeStruct((heads, 1, D), f32),
+            jax.ShapeDtypeStruct((1, CONV, NC), f32),
+            jax.ShapeDtypeStruct((1, CONV, 2 * S), f32),
+            jax.ShapeDtypeStruct((1, NC), f32),
+            jax.ShapeDtypeStruct((1, 2 * S), f32),
+            jax.ShapeDtypeStruct((1, heads), f32),
+            jax.ShapeDtypeStruct((1, heads), f32),
+            jax.ShapeDtypeStruct((1, heads), f32),
+            jax.ShapeDtypeStruct((1, NC), f32),
+            jax.ShapeDtypeStruct((1, NC, D), f32),
+        ),
+        in_specs=[any_] * 2 + [vmem] * 6,
+        out_specs=(any_,) * 2 + (vmem,) * 14,
+        scratch_shapes=[pltpu.SemaphoreType.DMA((2,))],
+        compiler_params=pltpu.CompilerParams(vmem_limit_bytes=40 * 1024 * 1024),
+    )(*made)
+    swap = {3: (0, 2, 1), 4: (0, 2, 1), 6: (1, 2, 0)}
+    done = [x.reshape(1, 2, T, D) for x in done[:2]] + list(done[2:])
+    return tuple(jnp.transpose(x, swap[i]) if i in swap else x for i, x in enumerate(done))
 
 
 def solution(mesh):
+    side = int(mesh.shape["tensor"] ** 0.5)
+    split = (side, mesh.shape["tensor"] // side)
     in_specs = (
         P(None, "dp", None),
         P(),
@@ -1050,7 +1232,7 @@
         P("pipe", "tensor", None),
     )
     return jax.shard_map(
-        functools.partial(on_device, (mesh.shape["tensor"], mesh.shape["dp"])),
+        functools.partial(on_device, (split, mesh.shape["dp"])),
         mesh=mesh,
         in_specs=in_specs,
         out_specs=out_specs,

time: 199 us -> 158 us (0.79)
  Pallas kernels: 176 us -> 146 us
  local copies, waits for them, and re-layouts: 19.6 us -> 10 us
  other arithmetic: 3.03 us -> 0 us
    pallas_call x1 -> x2, Pallas kernels: 176 us -> 146 us  [the longest x1 142 us: on_device(): pl.pallas_call(functools.partial(kernel, (T, D, NC, S, TZ, TX, DP), names...]
    slice x3 -> x0, local copies, waits for them, and re-layouts: 3.99 us -> none  [the longest x1 1.42 us: on_device(): pack[13:14, 0:NC]]
    unnamed x25 -> x16, local copies, waits for them, and re-layouts: 12.3 us -> 8.7 us
    broadcast_in_dim x3 -> x0, local copies, waits for them, and re-layouts: 2.59 us -> none  [the longest x1 1.29 us: on_device(): pack[8:12, 0:NC][None]]
    convert_element_type x2 -> x0, other arithmetic: 2.41 us -> none  [the longest x1 1.26 us: on_device(): dwbc.astype(f32)]
where the time goes in v2:
time: 158 us; the launch traced here: 157 us
  Pallas kernels  146 us (92%)
  local copies, waits for them, and re-layouts  10 us (6%)
    pallas_call x1, Pallas kernels, on_device(): pl.pallas_call(functools.partial(kernel, (T, D, NC, S, TZ, TX, DP), names...  142 us
    unnamed x16, local copies, waits for them, and re-layouts  8.7 us
    pallas_call x1, Pallas kernels, on_device(): pl.pallas_call(functools.partial(finish, (T, D, NC, S)), out_shape=(jax.S...  4.03 us

profile of v2, /device:TPU:0, one launch (start us, length us, event | category | flops | bytes accessed | tf_op | source)
XLA Modules:
  0.0 157.1 jit_solution(10063713128682007467)
XLA Ops:
  0.6 1.3 pad.4.refs_5_
  2.0 142.2 %shard_map.288 = (bf16[1,2,4,4,16,1536]{5,4,3,2,1,0:T(8,128)(2,1)}, bf16[1,2,4,4,16,1536]{5,4,3,2,1,0:T(8,128)(2,1)}, bf16[1,192,1536]{2,1,0:T(8,128)(2,1)}, bf1...) custom-call(bf16[2,4,4,16,1536]{4,3,2,1,0:T(8,128)(2,1)} %bitcast.10, ...), custom_call_target="tpu_custom_call" | custom-call | tf_op jit(solution)/shard_map/pallas_call | solution.py:1144
  144.2 0.0 copy-start
  144.2 1.4 copy-done
  145.6 0.0 copy-start.1
  145.6 1.4 copy-done.1
  147.0 0.0 copy-start.2
  147.0 1.1 copy-done.2
  148.1 0.0 copy-start.3
  148.1 1.1 copy-done.3
  149.2 0.0 copy-start.4
  149.2 1.1 copy-done.4
  150.2 0.0 copy-start.5
  150.2 1.1 copy-done.5
  151.3 0.0 copy-start.6
  151.3 0.8 copy-done.6
  152.1 0.0 copy-start.7
  152.1 0.8 copy-done.7
  152.9 4.0 %shard_map.289 = (bf16[1,2,4,4,16,1536]{5,4,3,2,1,0:T(8,128)(2,1)}, bf16[1,2,4,4,16,1536]{5,4,3,2,1,0:T(8,128)(2,1)}, f32[1,1536]{1,0:T(1,128)}, f32[1,192,1536]...) custom-call(bf16[1,2,4,4,16,1536]{5,4,3,2,1,0:T(8,128)(2,1)S(1)} %co, ...), custom_call_target="tpu_custom_call" | custom-call | tf_op jit(solution)/shard_map/pallas_call | solution.py:1164
Async XLA Ops:
  144.2 1.4 copy-start
  145.6 1.4 copy-start.1
  147.0 1.1 copy-start.2
  148.1 1.1 copy-start.3
  149.2 1.1 copy-start.4
  150.2 1.1 copy-start.5
  151.3 0.8 copy-start.6
  152.1 0.8 copy-start.7
